TPU v7x, 32 devices: a whole 2x2x4 slice. The times are simulated.
32 devices in a mesh: tm: 4 (over y, x), clus: 8 (over z, core).
Axes of the slice: x: 2, y: 2, z: 4, core: 2. Of those that a mesh axis runs over, the one named last changes fastest.
Arguments:
- currents: bfloat16 [256, 256, 128], P('clus', 'tm'), may hold values from -6 to 6
- excitation: bfloat16 [256, 256, 128], P('clus', 'tm'), may hold values from -6 to 6
- neighbours: int32 [256, 30], P('clus'), may hold values from -1 to 255, as said below
- lag_profile: bfloat16 [30, 64], replicated, may hold values from -0.125 to 0.125
- couplings: bfloat16 [30, 128, 128], replicated, may hold values from -0.5 to 0.5
- block_inverses: bfloat16 [256, 128, 128], P('clus'), may hold values from -0.5 to 0.5
- charge_map: bfloat16 [128, 128], replicated, may hold values from -0.03125 to 0.03125
- potential: bfloat16 [128, 128], replicated, may hold values from -0.5 to 0.5
Outputs:
- updated: bfloat16 [256, 256, 128], P('clus', 'tm')
- residual: float32 [256, 256, 128], P('clus', 'tm')
Inputs may be any that keep to these rules, and one draw needn't show every extreme that they name: `neighbours`: row j lists distinct panel clusters from j // 32 * 32 - 32 to j // 32 * 32 + 2 * 32 - 1, modulo 256; entries -1 pad the end of a row, and every row has a cluster in its first slot.
All inputs are finite; a program needn't handle non-finite values.
Results may differ from a plain program's by a relative error of at most 0.0051.
Values may be sent and summed in bfloat16 or wider, within the bound.
A program may use at most 64 MiB of HBM per device.

v0:
```python
import math

import jax
import jax.numpy as jnp
from jax import lax
from jax.sharding import PartitionSpec as P


def from_behind(x, axis, by):
    peers = lax.axis_size(axis)
    pairs = [(i, i + by) for i in range(peers) if 0 <= i + by < peers]
    return lax.ppermute(x, axis, pairs)


def with_halo(x, sides, width):
    for axis, dim in sides:
        peers, length = (lax.axis_size(axis), x.shape[dim])
        up = [(i, (i + 1) % peers) for i in range(peers)]
        down = [(j, i) for i, j in up]
        last = lax.slice_in_dim(x, length - width, length, axis=dim)
        first = lax.slice_in_dim(x, 0, width, axis=dim)
        before = lax.ppermute(last, axis, up)
        after = lax.ppermute(first, axis, down)
        x = jnp.concatenate([before, x, after], axis=dim)
    return x


def entering(value, axis, join, neutral):
    count, mine = (lax.axis_size(axis), lax.axis_index(axis))
    pieces = lax.all_gather(value, axis)
    so_far = jnp.full_like(value, 0) + jnp.asarray(neutral, value.dtype)

    def lap(position, so_far):
        longer = join(so_far, pieces[position])
        return jnp.where(position < mine, longer, so_far)

    return lax.fori_loop(0, count - 1, lap, so_far)


def add_terms(earlier, later):
    return earlier + later


def on_device(
    currents, excitation, neighbours, lag_profile, couplings, block_inverses, charge_map, potential
):
    per_dev, steps_block, unknowns = currents.shape
    slot_count, lag_count = lag_profile.shape
    window = steps_block + lag_count
    cluster_total = per_dev * lax.axis_size("clus")
    previous = from_behind(currents, "tm", 1)
    joined = jnp.concatenate([previous, currents], axis=1)
    extended = with_halo(joined, (("clus", 0),), per_dev)
    first_local = (lax.axis_index("clus") - 1) * per_dev
    present = neighbours >= 0
    local_ids = jnp.where(present, (neighbours - first_local) % cluster_total, 0)
    present_f = present.astype(jnp.float32)
    lag_index = jnp.arange(steps_block)[:, None] + lag_count - jnp.arange(window)[None, :]
    lag_onehot = (lag_index[:, :, None] == jnp.arange(lag_count)[None, None, :]).astype(
        jnp.bfloat16
    )
    toeplitz = jnp.einsum(
        "kl,tsl->kts", lag_profile, lag_onehot, preferred_element_type=jnp.float32
    ).astype(jnp.bfloat16)
    per_group = math.gcd(slot_count, 6)
    group_count = slot_count // per_group
    slot_ids = local_ids.T.reshape(group_count, per_group, per_dev)
    slot_mask = present_f.T.reshape(group_count, per_group, per_dev)
    slot_toep = toeplitz.reshape(group_count, per_group, steps_block, window)
    slot_coup = couplings.reshape(group_count, per_group, unknowns, unknowns)

    def add_group(accum, pieces):
        group_ids, group_mask, group_toep, group_coup = pieces
        gathered = jnp.take(extended, group_ids, axis=0)
        filtered = jnp.einsum(
            "kts,kcsb->kctb", group_toep, gathered, preferred_element_type=jnp.float32
        )
        filtered = (filtered * group_mask[:, :, None, None]).astype(jnp.bfloat16)
        return (
            accum
            + jnp.einsum("kctb,kbd->ctd", filtered, group_coup, preferred_element_type=jnp.float32),
            None,
        )

    start_field = jnp.zeros((per_dev, steps_block, unknowns), jnp.float32)
    near_field, _ = lax.scan(add_group, start_field, (slot_ids, slot_mask, slot_toep, slot_coup))
    increments = jnp.dot(
        currents.reshape(-1, unknowns), charge_map, preferred_element_type=jnp.float32
    )
    increments = increments.reshape(per_dev, steps_block, -1)
    totals = jnp.sum(increments, axis=1)
    before = entering(totals, "tm", add_terms, jnp.zeros_like(totals))
    lower_ones = (jnp.arange(steps_block)[:, None] >= jnp.arange(steps_block)[None, :]).astype(
        jnp.float32
    )
    running = jnp.einsum("ts,csm->ctm", lower_ones, increments, precision=lax.Precision.HIGHEST)
    charge = (before[:, None, :] + running).astype(jnp.bfloat16)
    charge_field = jnp.dot(
        charge.reshape(per_dev * steps_block, -1), potential, preferred_element_type=jnp.float32
    )
    charge_field = charge_field.reshape(per_dev, steps_block, unknowns)
    residual = excitation.astype(jnp.float32) - near_field - charge_field
    correction = jnp.einsum(
        "ctb,cbd->ctd",
        residual.astype(jnp.bfloat16),
        block_inverses,
        preferred_element_type=jnp.float32,
    )
    updated = (currents.astype(jnp.float32) + correction).astype(jnp.bfloat16)
    return (updated, residual)


def solution(mesh):
    in_specs = (
        P("clus", "tm", None),
        P("clus", "tm", None),
        P("clus", None),
        P(),
        P(),
        P("clus", None, None),
        P(),
        P(),
    )
    out_specs = (P("clus", "tm", None), P("clus", "tm", None))
    return jax.shard_map(
        on_device, mesh=mesh, in_specs=in_specs, out_specs=out_specs, check_vma=False
    )
```

profile of v0, /device:TPU:5, one launch (start us, length us, event | category | flops | bytes accessed | tf_op | source)
XLA Modules:
  0.0 136.5 jit_solution(16824076274041534023)
XLA Ops:
  0.6 0.0 copy-start
  0.6 0.0 copy-start.4
  0.7 3.3 %collective-permute-start = (bf16[32,64,128]{2,1,0:T(8,128)(2,1)}, bf16[32,64,128]{2,1,0:T(8,128)(2,1)S(1)}, u32[]{:S(2)}, u32[]{:S(2)}) collective-permute-start(bf16[32,64,128]{2,1,0:T(8,128)(2,1)} %param.12), channel_id=1, source_target_pairs={{0,8},{8,16},{16,24},{1,9},{9,17},{17,25},{2,10},{10,18},{18,26},{... | collective-permute-start | bytes 1572872 | tf_op jit(solution)/shard_map/ppermute | solution.py:12
  3.9 0.1 iota_subtract_fusion
  4.0 1.2 fusion.32
  5.2 0.7 fusion.44
  5.9 0.1 copy.12
  6.0 1.0 copy.13
  7.0 0.7 convert_bitcast_fusion
  7.7 0.1 copy.14
  7.8 1.3 fusion.46
  9.1 9.0 %all-gather = f32[128,128]{1,0:T(8,128)S(1)} all-gather(f32[32,128]{1,0:T(8,128)S(1)} %get-tuple-element.195), channel_id=2, replica_groups=mesh['tm'=4,'clus'=8] {'tm'}, dimensions={0}, use_global_device_ids=true | all-gather | bytes 81920 | tf_op jit(solution)/shard_map/all_gather | solution.py:30
  18.2 0.0 collective-permute-done
  18.2 0.9 constant_dynamic-update-slice_fusion.1
  19.1 1.9 %constant_dynamic-update-slice_fusion = bf16[32,128,128]{2,1,0:T(8,128)(2,1)} fusion(bf16[32,128,128]{2,1,0:T(8,128)(2,1)} %constant_dynamic-update-slice_fusion.1, bf16[32,64,128]{2,1,0:T(8,128)(2,1)} %param.12), kind=kLoop, calls=%fused_computation.50 | loop fusion | bytes 1048576 | tf_op jit(solution)/shard_map/concatenate | solution.py:52
  21.0 3.8 %collective-permute-start.1 = (bf16[32,128,128]{2,1,0:T(8,128)(2,1)}, bf16[32,128,128]{2,1,0:T(8,128)(2,1)S(1)}, u32[]{:S(2)}, u32[]{:S(2)}) collective-permute-start(bf16[32,128,128]{2,1,0:T(8,128)(2,1)} %constant_dynamic-update-slice_fusion), channel_id=1, source_target_pairs={{0,1},{1,2},{2,3},{3,4},{4,5},{5,6},{6,7},{7,0},{8,9},{9,10},{10,1... | collective-permute-start | bytes 3145736 | tf_op jit(solution)/shard_map/ppermute | solution.py:22
  24.9 0.0 collective-permute-start.2
  24.9 0.1 while.26
  25.0 0.7 fusion.33
  25.7 0.3 fusion.36
  26.0 19.6 %collective-permute-done.1 = bf16[32,128,128]{2,1,0:T(8,128)(2,1)S(1)} collective-permute-done((bf16[32,128,128]{2,1,0:T(8,128)(2,1)}, bf16[32,128,128]{2,1,0:T(8,128)(2,1)S(1)}, u32[]{:S(2)}, u32[]{:S(2)}) %collective-permute-start.1) | collective-permute-done | bytes 1048608 | tf_op jit(solution)/shard_map/ppermute | solution.py:22
  45.5 5.0 %collective-permute-done.2 = bf16[32,128,128]{2,1,0:T(8,128)(2,1)} collective-permute-done((bf16[32,128,128]{2,1,0:T(8,128)(2,1)}, bf16[32,128,128]{2,1,0:T(8,128)(2,1)}, u32[]{:S(2)}, u32[]{:S(2)}) %collective-permute-start.2) | collective-permute-done | bytes 1048608 | tf_op jit(solution)/shard_map/ppermute | solution.py:23
  50.6 3.1 %pad_maximum_fusion = bf16[96,128,128]{2,1,0:T(8,128)(2,1)} fusion(bf16[32,128,128]{2,1,0:T(8,128)(2,1)} %collective-permute-done.2, bf16[32,128,128]{2,1,0:T(8,128)(2,1)} %constant_dynamic-update-slice_fusion, bf16[32,128,128]{2,1,0:T(8,128)(2,1)S(1)} %collective-permute-done.1), kind=kLoop, calls=%fused_computation.21 | loop fusion | flops 3145728 | bytes 6291456 | tf_op jit(solution)/shard_map/concatenate | solution.py:24
  53.6 80.1 %while.25 = (s32[]{:T(128)}, f32[32,64,128]{2,1,0:T(8,128)}, s32[5,6,32]{2,1,0:T(8,128)S(1)}, bf16[96,128,128]{2,1,0:T(8,128)(2,1)}, bf16[5,6,64,128]{3,2,1,0:T(...) while((s32[]{:T(128)}, f32[32,64,128]{2,1,0:T(8,128)}, ...), condition=%wide.region_1.2_spmd.clone, body=%wide.region_0.1_spmd.clone.sunk | while | flops 812124864 | bytes 21281268 | solution.py:86
  53.6 0.1 reshape.124
  53.7 10.0 %gather_fusion = bf16[192,128,128]{2,1,0:T(8,128)(2,1)} fusion(bf16[96,128,128]{2,1,0:T(8,128)(2,1)} %get-tuple-element.304, s32[1024]{0:T(1024)S(1)} %pad_clamp_fusion.2), kind=kCustom, calls=%fused_computation.clone.clone.1 | custom fusion | bytes 12583680 | tf_op jit(solution)/shard_map/while/body/eval_jaxpr/jit(_take)/gather | solution.py:74
  63.8 0.1 copy.32
  63.9 5.7 %fusion.60 = f32[32,64,128]{2,1,0:T(8,128)} fusion(f32[6,32]{0,1:T(8,128)S(1)} %bitcast.82, f32[32,64,128]{2,1,0:T(8,128)} %get-tuple-element.293, pred[]{:T(512)S(6)} %compare.7, bf16[5,6,128,128]{3,2,1,0:T(8,128)(2,1)} %get-tuple-element.307, s32[]{:T(128)} %get-tuple-element.292, bf16[5,6,64,128]{3,2,1,0:T(8,128)(2,1)} %get-tuple-element.305, ...), kind=kOutput, calls=%fused_computation.9.clone.1 | convolution fusion | flops 812122112 | bytes 8685505 | tf_op jit(solution)/shard_map/while/body/eval_jaxpr/kctb,kbd->ctd/dot_general | solution.py:81
  69.6 0.1 reshape.124
  69.7 10.0 %gather_fusion = bf16[192,128,128]{2,1,0:T(8,128)(2,1)} fusion(bf16[96,128,128]{2,1,0:T(8,128)(2,1)} %get-tuple-element.304, s32[1024]{0:T(1024)S(1)} %pad_clamp_fusion.2), kind=kCustom, calls=%fused_computation.clone.clone.1 | custom fusion | bytes 12583680 | tf_op jit(solution)/shard_map/while/body/eval_jaxpr/jit(_take)/gather | solution.py:74
  79.7 0.1 copy.32
  79.8 5.9 %fusion.60 = f32[32,64,128]{2,1,0:T(8,128)} fusion(f32[6,32]{0,1:T(8,128)S(1)} %bitcast.82, f32[32,64,128]{2,1,0:T(8,128)} %get-tuple-element.293, pred[]{:T(512)S(6)} %compare.7, bf16[5,6,128,128]{3,2,1,0:T(8,128)(2,1)} %get-tuple-element.307, s32[]{:T(128)} %get-tuple-element.292, bf16[5,6,64,128]{3,2,1,0:T(8,128)(2,1)} %get-tuple-element.305, ...), kind=kOutput, calls=%fused_computation.9.clone.1 | convolution fusion | flops 812122112 | bytes 8685505 | tf_op jit(solution)/shard_map/while/body/eval_jaxpr/kctb,kbd->ctd/dot_general | solution.py:81
  85.7 0.1 reshape.124
  85.8 10.0 %gather_fusion = bf16[192,128,128]{2,1,0:T(8,128)(2,1)} fusion(bf16[96,128,128]{2,1,0:T(8,128)(2,1)} %get-tuple-element.304, s32[1024]{0:T(1024)S(1)} %pad_clamp_fusion.2), kind=kCustom, calls=%fused_computation.clone.clone.1 | custom fusion | bytes 12583680 | tf_op jit(solution)/shard_map/while/body/eval_jaxpr/jit(_take)/gather | solution.py:74
  95.7 0.1 copy.32
  95.8 5.9 %fusion.60 = f32[32,64,128]{2,1,0:T(8,128)} fusion(f32[6,32]{0,1:T(8,128)S(1)} %bitcast.82, f32[32,64,128]{2,1,0:T(8,128)} %get-tuple-element.293, pred[]{:T(512)S(6)} %compare.7, bf16[5,6,128,128]{3,2,1,0:T(8,128)(2,1)} %get-tuple-element.307, s32[]{:T(128)} %get-tuple-element.292, bf16[5,6,64,128]{3,2,1,0:T(8,128)(2,1)} %get-tuple-element.305, ...), kind=kOutput, calls=%fused_computation.9.clone.1 | convolution fusion | flops 812122112 | bytes 8685505 | tf_op jit(solution)/shard_map/while/body/eval_jaxpr/kctb,kbd->ctd/dot_general | solution.py:81
  101.7 0.1 reshape.124
  101.8 10.0 %gather_fusion = bf16[192,128,128]{2,1,0:T(8,128)(2,1)} fusion(bf16[96,128,128]{2,1,0:T(8,128)(2,1)} %get-tuple-element.304, s32[1024]{0:T(1024)S(1)} %pad_clamp_fusion.2), kind=kCustom, calls=%fused_computation.clone.clone.1 | custom fusion | bytes 12583680 | tf_op jit(solution)/shard_map/while/body/eval_jaxpr/jit(_take)/gather | solution.py:74
  111.8 0.1 copy.32
  111.9 5.9 %fusion.60 = f32[32,64,128]{2,1,0:T(8,128)} fusion(f32[6,32]{0,1:T(8,128)S(1)} %bitcast.82, f32[32,64,128]{2,1,0:T(8,128)} %get-tuple-element.293, pred[]{:T(512)S(6)} %compare.7, bf16[5,6,128,128]{3,2,1,0:T(8,128)(2,1)} %get-tuple-element.307, s32[]{:T(128)} %get-tuple-element.292, bf16[5,6,64,128]{3,2,1,0:T(8,128)(2,1)} %get-tuple-element.305, ...), kind=kOutput, calls=%fused_computation.9.clone.1 | convolution fusion | flops 812122112 | bytes 8685505 | tf_op jit(solution)/shard_map/while/body/eval_jaxpr/kctb,kbd->ctd/dot_general | solution.py:81
  117.8 0.1 reshape.124
  117.9 9.9 %gather_fusion = bf16[192,128,128]{2,1,0:T(8,128)(2,1)} fusion(bf16[96,128,128]{2,1,0:T(8,128)(2,1)} %get-tuple-element.304, s32[1024]{0:T(1024)S(1)} %pad_clamp_fusion.2), kind=kCustom, calls=%fused_computation.clone.clone.1 | custom fusion | bytes 12583680 | tf_op jit(solution)/shard_map/while/body/eval_jaxpr/jit(_take)/gather | solution.py:74
  127.8 0.1 copy.32
  127.9 5.9 %fusion.60 = f32[32,64,128]{2,1,0:T(8,128)} fusion(f32[6,32]{0,1:T(8,128)S(1)} %bitcast.82, f32[32,64,128]{2,1,0:T(8,128)} %get-tuple-element.293, pred[]{:T(512)S(6)} %compare.7, bf16[5,6,128,128]{3,2,1,0:T(8,128)(2,1)} %get-tuple-element.307, s32[]{:T(128)} %get-tuple-element.292, bf16[5,6,64,128]{3,2,1,0:T(8,128)(2,1)} %get-tuple-element.305, ...), kind=kOutput, calls=%fused_computation.9.clone.1 | convolution fusion | flops 812122112 | bytes 8685505 | tf_op jit(solution)/shard_map/while/body/eval_jaxpr/kctb,kbd->ctd/dot_general | solution.py:81
  133.8 0.0 copy-done.3
  133.8 1.5 %subtract_subtract_fusion = f32[32,64,128]{2,1,0:T(8,128)S(1)} fusion(f32[32,64,128]{2,1,0:T(8,128)S(1)} %fusion.36, f32[32,64,128]{2,1,0:T(8,128)} %get-tuple-element.118, bf16[32,64,128]{2,1,0:T(8,128)(2,1)S(1)} %copy-done.3), kind=kLoop, calls=%fused_computation.31 | loop fusion | flops 786432 | bytes 3670016 | tf_op jit(solution)/shard_map/sub | solution.py:102
  135.2 0.0 copy-start.2
  135.3 1.2 fusion.29
  (34 shorter events, 0.2 us)
Async XLA Ops:
  0.6 134.6 %copy-start = (bf16[32,128,128]{2,1,0:T(8,128)(2,1)S(1)}, bf16[32,128,128]{2,1,0:T(8,128)(2,1)}, u32[]{:S(2)}) copy-start(bf16[32,128,128]{2,1,0:T(8,128)(2,1)} %param.17) | copy-start | bytes 3145732
  0.6 25.0 %copy-start.4 = (bf16[128,128]{1,0:T(8,128)(2,1)S(1)}, bf16[128,128]{1,0:T(8,128)(2,1)}, u32[]{:S(2)}) copy-start(bf16[128,128]{1,0:T(8,128)(2,1)} %param.19) | copy-start | bytes 98308
  0.7 17.5 %collective-permute-start = (bf16[32,64,128]{2,1,0:T(8,128)(2,1)}, bf16[32,64,128]{2,1,0:T(8,128)(2,1)S(1)}, u32[]{:S(2)}, u32[]{:S(2)}) collective-permute-start(bf16[32,64,128]{2,1,0:T(8,128)(2,1)} %param.12), channel_id=1, source_target_pairs={{0,8},{8,16},{16,24},{1,9},{9,17},{17,25},{2,10},{10,18},{18,26},{... | collective-permute-start | bytes 1572872 | tf_op jit(solution)/shard_map/ppermute | solution.py:12
  21.0 24.5 %collective-permute-start.1 = (bf16[32,128,128]{2,1,0:T(8,128)(2,1)}, bf16[32,128,128]{2,1,0:T(8,128)(2,1)S(1)}, u32[]{:S(2)}, u32[]{:S(2)}) collective-permute-start(bf16[32,128,128]{2,1,0:T(8,128)(2,1)} %constant_dynamic-update-slice_fusion), channel_id=1, source_target_pairs={{0,1},{1,2},{2,3},{3,4},{4,5},{5,6},{6,7},{7,0},{8,9},{9,10},{10,1... | collective-permute-start | bytes 3145736 | tf_op jit(solution)/shard_map/ppermute | solution.py:22
  24.9 25.7 %collective-permute-start.2 = (bf16[32,128,128]{2,1,0:T(8,128)(2,1)}, bf16[32,128,128]{2,1,0:T(8,128)(2,1)}, u32[]{:S(2)}, u32[]{:S(2)}) collective-permute-start(bf16[32,128,128]{2,1,0:T(8,128)(2,1)} %constant_dynamic-update-slice_fusion), channel_id=1, source_target_pairs={{1,0},{2,1},{3,2},{4,3},{5,4},{6,5},{7,6},{0,7},{9,8},{10,9},{11,1... | collective-permute-start | bytes 3145736 | tf_op jit(solution)/shard_map/ppermute | solution.py:23
  53.6 80.1 %copy-start.3 = (bf16[32,64,128]{2,1,0:T(8,128)(2,1)S(1)}, bf16[32,64,128]{2,1,0:T(8,128)(2,1)}, u32[]{:S(2)}) copy-start(bf16[32,64,128]{2,1,0:T(8,128)(2,1)} %param.13) | copy-start | bytes 1572868
  53.6 81.6 %copy-start.1 = (bf16[32,64,128]{2,1,0:T(8,128)(2,1)S(1)}, bf16[32,64,128]{2,1,0:T(8,128)(2,1)}, u32[]{:S(2)}) copy-start(bf16[32,64,128]{2,1,0:T(8,128)(2,1)} %param.12) | copy-start | bytes 1572868
  135.2 1.2 copy-start.2
where the time goes:
time: 138 us; the launch traced here: 136 us
  local copies, waits for them, and re-layouts  54.7 us (40%)
  matrix products  34.1 us (25%)
  waiting for transfers between devices  24.6 us (18%)
  blocking collectives  9.05 us (7%)
  starting transfers between devices  7.07 us (5%)
  other arithmetic  6.19 us (4%)
    gather x5, local copies, waits for them, and re-layouts, add_group(): gathered = jnp.take(extended, group_ids, axis=0)  49.8 us
    dot_general x5, matrix products, add_group(): jnp.einsum('kctb,kbd->ctd', filtered, group_coup, preferred_element_type=...  29.4 us
    ppermute x1, waiting for transfers between devices, with_halo(): before = lax.ppermute(last, axis, up)  19.6 us
    all_gather x1, blocking collectives, entering(): pieces = lax.all_gather(value, axis)  9.05 us
    ppermute x1, waiting for transfers between devices, with_halo(): after = lax.ppermute(first, axis, down)  5.02 us
    ppermute x1, starting transfers between devices, with_halo(): before = lax.ppermute(last, axis, up)  3.82 us
    ppermute x1, starting transfers between devices, from_behind(): return lax.ppermute(x, axis, pairs)  3.25 us
    concatenate x1, other arithmetic, with_halo(): x = jnp.concatenate([before, x, after], axis=dim)  3.08 us
  transfers between devices with their start and end apart: 3, of which 2 were waited for; matrix products, arithmetic and copies ran while one was open for 5% of the time, Pallas kernels for 0%

commit v1 on v0

v1 whole, which is shorter than its diff:
```python
import jax
import jax.numpy as jnp
from jax import lax
from jax.experimental import pallas as pl
from jax.experimental.pallas import tpu as pltpu
from jax.sharding import PartitionSpec as P

GROUP = 4


def sweep_kernel(
    ids, own, prev, left, left_prev, right, right_prev, exc, toep, coup, binv, cmap, pot, before,
    upd, res, ext, filt, lower, sems,
):
    group = pl.program_id(0)
    per_dev, steps, unknowns = own.shape
    slots, _, window = toep.shape
    lags = window - steps

    @pl.when(group == 0)
    def _():
        copies = []
        for n, (old, new) in enumerate(((left_prev, left), (prev, own), (right_prev, right))):
            rows = pl.ds(n * per_dev, per_dev)
            copies.append(
                pltpu.make_async_copy(old, ext.at[rows, pl.ds(0, lags)], sems.at[2 * n])
            )
            copies.append(
                pltpu.make_async_copy(new, ext.at[rows, pl.ds(lags, steps)], sems.at[2 * n + 1])
            )
        for copy in copies:
            copy.start()
        ext[3 * per_dev] = jnp.zeros((window, unknowns), ext.dtype)
        size = GROUP * steps
        row = lax.broadcasted_iota(jnp.int32, (size, size), 0)
        col = lax.broadcasted_iota(jnp.int32, (size, size), 1)
        keep = (row >= col) & (row // steps == col // steps)
        lower[...] = jnp.where(keep, 1.0, 0.0).astype(lower.dtype)
        for copy in copies:
            copy.wait()

    first = group * GROUP
    for k in range(slots):
        for c in range(0, GROUP, 2):
            one = ext[ids[first + c, k]]
            two = ext[ids[first + c + 1, k]]
            both = jnp.concatenate([one, two], axis=1)
            out = jnp.dot(toep[k], both, preferred_element_type=jnp.float32)
            out = out.astype(jnp.bfloat16)
            lanes = pl.ds(k * unknowns, unknowns)
            filt[pl.ds(c * steps, steps), lanes] = out[:, :unknowns]
            filt[pl.ds((c + 1) * steps, steps), lanes] = out[:, unknowns:]
    near = jnp.dot(filt[...], coup[...], preferred_element_type=jnp.float32)

    own_rows = ext[pl.ds(per_dev + first, GROUP), pl.ds(lags, steps)]
    own_rows = own_rows.reshape(GROUP * steps, unknowns)
    incr = jnp.dot(own_rows, cmap[...], preferred_element_type=jnp.float32)
    high = incr.astype(jnp.bfloat16)
    rest = (incr - high.astype(jnp.float32)).astype(jnp.bfloat16)
    sums = jnp.dot(
        lower[...], jnp.concatenate([high, rest], axis=1), preferred_element_type=jnp.float32
    )
    patches = incr.shape[1]
    running = (sums[:, :patches] + sums[:, patches:]).reshape(GROUP, steps, patches)
    charge = (running + before[...][:, None, :]).astype(jnp.bfloat16)
    field = jnp.dot(
        charge.reshape(GROUP * steps, patches), pot[...], preferred_element_type=jnp.float32
    )
    residual = (
        exc[...].astype(jnp.float32).reshape(GROUP * steps, unknowns) - near - field
    )
    res[...] = residual.reshape(GROUP, steps, unknowns)
    rounded = residual.astype(jnp.bfloat16)
    for c in range(GROUP):
        rows = slice(c * steps, (c + 1) * steps)
        step = jnp.dot(rounded[rows], binv[c], preferred_element_type=jnp.float32)
        upd[c] = (own_rows[rows].astype(jnp.float32) + step).astype(upd.dtype)


def on_device(
    currents, excitation, neighbours, lag_profile, couplings, block_inverses, charge_map, potential
):
    per_dev, steps, unknowns = currents.shape
    slots, lags = lag_profile.shape
    window = steps + lags
    patches = charge_map.shape[1]
    n_tm, n_clus = lax.axis_size("tm"), lax.axis_size("clus")
    total = per_dev * n_clus

    def sent(x, by_tm, by_clus):
        pairs = [
            (t * n_clus + c, (t + by_tm) * n_clus + (c + by_clus) % n_clus)
            for t in range(n_tm - by_tm)
            for c in range(n_clus)
        ]
        return lax.ppermute(x, ("tm", "clus"), pairs)

    left = sent(currents, 0, 1)
    right = sent(currents, 0, -1)
    left_prev = sent(currents, 1, 1)
    right_prev = sent(currents, 1, -1)
    prev = sent(currents, 1, 0)

    totals = jnp.dot(
        jnp.sum(currents.astype(jnp.float32), axis=1),
        charge_map.astype(jnp.float32),
        precision=lax.Precision.HIGHEST,
    )
    before = jnp.zeros_like(totals)
    for by in range(1, n_tm):
        before = before + sent(totals, by, 0)

    first_local = (lax.axis_index("clus") - 1) * per_dev
    ids = jnp.where(neighbours >= 0, (neighbours - first_local) % total, 3 * per_dev)
    lag_index = jnp.arange(steps)[:, None] + lags - jnp.arange(window)[None, :]
    onehot = (lag_index[:, :, None] == jnp.arange(lags)[None, None, :]).astype(jnp.bfloat16)
    toep = jnp.einsum(
        "kl,tsl->kts", lag_profile, onehot, preferred_element_type=jnp.float32
    ).astype(jnp.bfloat16)

    anywhere = pl.BlockSpec(memory_space=pl.ANY)

    def whole(*shape):
        return pl.BlockSpec(shape, lambda g, ids: (0,) * len(shape))

    def grouped(*shape):
        return pl.BlockSpec((GROUP,) + shape, lambda g, ids: (g,) + (0,) * len(shape))

    size = GROUP * steps
    pairs = per_dev * slots * steps * unknowns
    return pl.pallas_call(
        sweep_kernel,
        grid_spec=pltpu.PrefetchScalarGridSpec(
            num_scalar_prefetch=1,
            grid=(per_dev // GROUP,),
            in_specs=[anywhere] * 6
            + [
                grouped(steps, unknowns),
                whole(slots, steps, window),
                whole(slots * unknowns, unknowns),
                grouped(unknowns, unknowns),
                whole(unknowns, patches),
                whole(patches, unknowns),
                pl.BlockSpec((None, GROUP, patches), lambda g, ids: (g, 0, 0)),
            ],
            out_specs=[grouped(steps, unknowns), grouped(steps, unknowns)],
            scratch_shapes=[
                pltpu.VMEM((3 * per_dev + 1, window, unknowns), jnp.bfloat16),
                pltpu.VMEM((size, slots * unknowns), jnp.bfloat16),
                pltpu.VMEM((size, size), jnp.bfloat16),
                pltpu.SemaphoreType.DMA((6,)),
            ],
        ),
        out_shape=[
            jax.ShapeDtypeStruct(currents.shape, jnp.bfloat16),
            jax.ShapeDtypeStruct(currents.shape, jnp.float32),
        ],
        compiler_params=pltpu.CompilerParams(vmem_limit_bytes=40 << 20),
        cost_estimate=pl.CostEstimate(
            flops=2 * pairs * (window + unknowns), bytes_accessed=8 << 20, transcendentals=0
        ),
    )(
        ids, currents, prev, left, left_prev, right, right_prev, excitation, toep,
        couplings.reshape(slots * unknowns, unknowns), block_inverses, charge_map, potential,
        before.reshape(per_dev // GROUP, GROUP, patches),
    )


def solution(mesh):
    in_specs = (
        P("clus", "tm", None),
        P("clus", "tm", None),
        P("clus", None),
        P(),
        P(),
        P("clus", None, None),
        P(),
        P(),
    )
    out_specs = (P("clus", "tm", None), P("clus", "tm", None))
    return jax.shard_map(
        on_device, mesh=mesh, in_specs=in_specs, out_specs=out_specs, check_vma=False
    )
```

time: 138 us -> 67 us (0.49)
  local copies, waits for them, and re-layouts: 54.7 us -> 2.47 us
  matrix products: 34.1 us -> 2.24 us
  Pallas kernels: 0 us -> 16.4 us
  blocking collectives: 9.05 us -> 0 us
  starting transfers between devices: 7.07 us -> 14.4 us
  other arithmetic: 6.19 us -> 1.31 us
  waiting for transfers between devices: 24.6 us -> 28.1 us
    gather x5 -> x0, local copies, waits for them, and re-layouts: 49.8 us -> none  [add_group(): gathered = jnp.take(extended, group_ids, axis=0)]
    dot_general x10 -> x2, matrix products: 34.1 us -> 2.24 us  [the longest x1 1.25 us: on_device(): jnp.einsum('kl,tsl->kts', lag_profile, onehot, preferred_element_type=jnp...]
    pallas_call x0 -> x1, Pallas kernels: none -> 16.4 us  [on_device(): pl.pallas_call(sweep_kernel, grid_spec=pltpu.PrefetchScalarGridSpec(num_s...]
    all_gather x1 -> x0, blocking collectives: 9.05 us -> none  [entering(): pieces = lax.all_gather(value, axis)]
    ppermute x3 -> x8, starting transfers between devices: 7.07 us -> 14.4 us  [sent(): return lax.ppermute(x, ('tm', 'clus'), pairs)]
    ppermute x3 -> x8, waiting for transfers between devices: 24.6 us -> 28.1 us  [sent(): return lax.ppermute(x, ('tm', 'clus'), pairs)]
    concatenate x1 -> x0, other arithmetic: 3.08 us -> none  [with_halo(): x = jnp.concatenate([before, x, after], axis=dim)]
    concatenate x1 -> x0, local copies, waits for them, and re-layouts: 1.94 us -> none  [on_device(): joined = jnp.concatenate([previous, currents], axis=1)]
  transfers between devices with their start and end apart: 3 -> 8, of which waited for: 2 -> 4; matrix products, arithmetic and copies ran while one was open for 5% -> 4% of each run, Pallas kernels for 0% -> 0%
where the time goes in v1:
time: 67 us; the launch traced here: 65.7 us
  waiting for transfers between devices  28.1 us (42%)
  Pallas kernels  16.4 us (24%)
  starting transfers between devices  14.4 us (21%)
  local copies, waits for them, and re-layouts  2.47 us (4%)
  matrix products  2.24 us (3%)
  other arithmetic  1.31 us (2%)
  between operations  0.83 us (1%)
    ppermute x8, waiting for transfers between devices, sent(): return lax.ppermute(x, ('tm', 'clus'), pairs)  28.1 us
    pallas_call x1, Pallas kernels, on_device(): pl.pallas_call(sweep_kernel, grid_spec=pltpu.PrefetchScalarGridSpec(num_s...  16.4 us
    ppermute x8, starting transfers between devices, sent(): return lax.ppermute(x, ('tm', 'clus'), pairs)  14.4 us
  transfers between devices with their start and end apart: 8, of which 4 were waited for; matrix products, arithmetic and copies ran while one was open for 4% of the time, Pallas kernels for 0%

profile of v1, /device:TPU:5, one launch (start us, length us, event | category | flops | bytes accessed | tf_op | source)
XLA Modules:
  0.0 65.7 jit_solution(3517031046990734160)
XLA Ops:
  0.6 0.0 copy-start
  0.6 0.0 copy-start.7
  0.7 0.0 copy-start.5
  0.7 1.2 %convert_reduce_fusion = f32[32,128]{1,0:T(8,128)S(1)} fusion(bf16[32,64,128]{2,1,0:T(8,128)(2,1)} %own.1), kind=kLoop, calls=%fused_computation.2 | loop fusion | flops 520192 | bytes 540672 | tf_op jit(solution)/shard_map/reduce_sum | solution.py:105
  1.9 0.0 copy-start.1
  1.9 0.0 copy-start.2
  1.9 0.0 copy-start.3
  1.9 0.0 copy-start.6
  1.9 1.0 %fusion.6 = f32[32,128]{1,0:T(8,128)S(1)} fusion(f32[32,128]{1,0:T(8,128)S(1)} %convert_reduce_fusion, bf16[128,128]{1,0:T(8,128)(2,1)} %cmap.1), kind=kOutput, calls=%fused_computation.15 | convolution fusion | flops 6291456 | bytes 65536 | tf_op jit(solution)/shard_map/dot_general | solution.py:104
  2.9 0.7 %collective-permute-start.7 = (f32[32,128]{1,0:T(8,128)S(1)}, f32[32,128]{1,0:T(8,128)S(1)}, u32[]{:S(2)}, u32[]{:S(2)}) collective-permute-start(f32[32,128]{1,0:T(8,128)S(1)} %fusion.6), channel_id=1, source_target_pairs={{0,24},{1,25},{2,26},{3,27},{4,28},{5,29},{6,30},{7,31}} | collective-permute-start | bytes 49160 | tf_op jit(solution)/shard_map/ppermute | solution.py:96
  3.6 1.3 %collective-permute-start.6 = (f32[32,128]{1,0:T(8,128)S(1)}, f32[32,128]{1,0:T(8,128)S(1)}, u32[]{:S(2)}, u32[]{:S(2)}) collective-permute-start(f32[32,128]{1,0:T(8,128)S(1)} %fusion.6), channel_id=1, source_target_pairs={{0,16},{1,17},{2,18},{3,19},{4,20},{5,21},{6,22},{7,23},{8,24},{9,... | collective-permute-start | bytes 49160 | tf_op jit(solution)/shard_map/ppermute | solution.py:96
  4.9 3.7 %collective-permute-start.5 = (f32[32,128]{1,0:T(8,128)S(1)}, f32[32,128]{1,0:T(8,128)S(1)}, u32[]{:S(2)}, u32[]{:S(2)}) collective-permute-start(f32[32,128]{1,0:T(8,128)S(1)} %fusion.6), channel_id=1, source_target_pairs={{0,8},{1,9},{2,10},{3,11},{4,12},{5,13},{6,14},{7,15},{8,16},{9,17... | collective-permute-start | bytes 49160 | tf_op jit(solution)/shard_map/ppermute | solution.py:96
  8.7 1.9 %collective-permute-start.4 = (bf16[32,64,128]{2,1,0:T(8,128)(2,1)}, bf16[32,64,128]{2,1,0:T(8,128)(2,1)S(1)}, u32[]{:S(2)}, u32[]{:S(2)}) collective-permute-start(bf16[32,64,128]{2,1,0:T(8,128)(2,1)} %own.1), channel_id=1, source_target_pairs={{0,15},{1,8},{2,9},{3,10},{4,11},{5,12},{6,13},{7,14},{8,23},{9,16... | collective-permute-start | bytes 1572872 | tf_op jit(solution)/shard_map/ppermute | solution.py:96
  10.6 2.9 %collective-permute-start.3 = (bf16[32,64,128]{2,1,0:T(8,128)(2,1)}, bf16[32,64,128]{2,1,0:T(8,128)(2,1)}, u32[]{:S(2)}, u32[]{:S(2)}) collective-permute-start(bf16[32,64,128]{2,1,0:T(8,128)(2,1)} %own.1), channel_id=1, source_target_pairs={{0,7},{1,0},{2,1},{3,2},{4,3},{5,4},{6,5},{7,6},{8,15},{9,8},{10,9... | collective-permute-start | bytes 1572872 | tf_op jit(solution)/shard_map/ppermute | solution.py:96
  13.5 0.1 iota_subtract_fusion
  13.5 0.0 collective-permute-done.7
  13.5 1.9 %collective-permute-start.2 = (bf16[32,64,128]{2,1,0:T(8,128)(2,1)}, bf16[32,64,128]{2,1,0:T(8,128)(2,1)}, u32[]{:S(2)}, u32[]{:S(2)}) collective-permute-start(bf16[32,64,128]{2,1,0:T(8,128)(2,1)} %own.1), channel_id=1, source_target_pairs={{0,9},{1,10},{2,11},{3,12},{4,13},{5,14},{6,15},{7,8},{8,17},{9,18... | collective-permute-start | bytes 1572872 | tf_op jit(solution)/shard_map/ppermute | solution.py:96
  15.5 0.0 collective-permute-done.6
  15.5 0.1 collective-permute-start.1
  15.5 0.0 collective-permute-done.5
  15.6 1.9 %collective-permute-start = (bf16[32,64,128]{2,1,0:T(8,128)(2,1)}, bf16[32,64,128]{2,1,0:T(8,128)(2,1)}, u32[]{:S(2)}, u32[]{:S(2)}) collective-permute-start(bf16[32,64,128]{2,1,0:T(8,128)(2,1)} %own.1), channel_id=1, source_target_pairs={{0,8},{1,9},{2,10},{3,11},{4,12},{5,13},{6,14},{7,15},{8,16},{9,17... | collective-permute-start | bytes 1572872 | tf_op jit(solution)/shard_map/ppermute | solution.py:96
  17.5 0.0 copy-done
  17.5 1.2 %fusion = bf16[64,128,30]{1,2,0:T(8,128)(2,1)} fusion(s32[64,128]{1,0:T(8,128)S(1)} %iota_subtract_fusion, bf16[30,64]{1,0:T(8,128)(2,1)S(1)} %copy-done), kind=kOutput, calls=%fused_computation.1 | convolution fusion | flops 31981568 | bytes 528128 | tf_op jit(solution)/shard_map/kl,tsl->kts/dot_general | solution.py:117
  18.7 1.2 %copy.14 = bf16[64,128,30]{1,0,2:T(8,128)(2,1)S(1)} copy(bf16[64,128,30]{1,2,0:T(8,128)(2,1)} %fusion) | data formatting | bytes 983040 | tf_op jit(solution)/shard_map/kl,tsl->kts/dot_general | solution.py:117
  20.0 0.0 copy-done.7
  20.0 11.5 %collective-permute-done.4.right_prev = bf16[32,64,128]{2,1,0:T(8,128)(2,1)S(1)} collective-permute-done((bf16[32,64,128]{2,1,0:T(8,128)(2,1)}, bf16[32,64,128]{2,1,0:T(8,128)(2,1)S(1)}, u32[]{:S(2)}, u32[]{:S(2)}) %collective-permute-start.4) | collective-permute-done | bytes 524320 | tf_op jit(solution)/shard_map/ppermute | solution.py:96
  31.6 0.5 collective-permute-done.3.right
  32.1 6.6 %collective-permute-done.2.left_prev = bf16[32,64,128]{2,1,0:T(8,128)(2,1)} collective-permute-done((bf16[32,64,128]{2,1,0:T(8,128)(2,1)}, bf16[32,64,128]{2,1,0:T(8,128)(2,1)}, u32[]{:S(2)}, u32[]{:S(2)}) %collective-permute-start.2) | collective-permute-done | bytes 524320 | tf_op jit(solution)/shard_map/ppermute | solution.py:96
  38.7 0.0 collective-permute-done.1.left
  38.7 9.4 %collective-permute-done.prev = bf16[32,64,128]{2,1,0:T(8,128)(2,1)} collective-permute-done((bf16[32,64,128]{2,1,0:T(8,128)(2,1)}, bf16[32,64,128]{2,1,0:T(8,128)(2,1)}, u32[]{:S(2)}, u32[]{:S(2)}) %collective-permute-start) | collective-permute-done | bytes 524320 | tf_op jit(solution)/shard_map/ppermute | solution.py:96
  48.1 0.0 copy-done.5
  48.1 0.0 copy-done.1
  48.1 0.0 copy-done.2
  48.1 0.0 copy-done.3
  48.1 0.0 copy-done.6
  48.1 0.0 copy-start.4
  48.1 1.2 %copy-done.4 = bf16[30,128,128]{2,1,0:T(8,128)(2,1)S(1)} copy-done((bf16[30,128,128]{2,1,0:T(8,128)(2,1)S(1)}, bf16[30,128,128]{2,1,0:T(8,128)(2,1)}, u32[]{:S(2)}) %copy-start.4) | copy-done | bytes 983064
  49.3 16.4 %shard_map.95 = (bf16[32,64,128]{2,1,0:T(8,128)(2,1)}, f32[32,64,128]{2,1,0:T(8,128)}) custom-call(s32[32,30]{1,0:T(8,128)S(1)} %fusion.4.ids, bf16[32,64,128]{2,1,0:T(8,128)(2,1)S(1)} %copy-done.1, bf16[32,64,128]{2,1,0:T(8,128)(2,1)} %collective-permute-done.prev, bf16[32,64,128]{2,1,0:T(8,128)(2,1)} %collective-permute-done.1.left, ...), custom_call_target="tpu_custom_call" | custom-call | flops 4026531840 | bytes 8388608 | tf_op jit(solution)/shard_map/pallas_call | solution.py:131
  (3 shorter events, 0.0 us)
Async XLA Ops:
  0.6 16.9 %copy-start = (bf16[30,64]{1,0:T(8,128)(2,1)S(1)}, bf16[30,64]{1,0:T(8,128)(2,1)}, u32[]{:S(2)}) copy-start(bf16[30,64]{1,0:T(8,128)(2,1)} %param.11) | copy-start | bytes 11524
  0.6 19.3 %copy-start.7 = (s32[32,30]{1,0:T(8,128)S(1)}, s32[32,30]{1,0:T(8,128)}, u32[]{:S(2)}) copy-start(s32[32,30]{1,0:T(8,128)} %param.10) | copy-start | bytes 11524
  0.7 47.4 %copy-start.5 = (bf16[32,64,128]{2,1,0:T(8,128)(2,1)S(1)}, bf16[32,64,128]{2,1,0:T(8,128)(2,1)}, u32[]{:S(2)}) copy-start(bf16[32,64,128]{2,1,0:T(8,128)(2,1)} %exc.1) | copy-start | bytes 1572868
  1.9 46.2 %copy-start.1 = (bf16[32,64,128]{2,1,0:T(8,128)(2,1)S(1)}, bf16[32,64,128]{2,1,0:T(8,128)(2,1)}, u32[]{:S(2)}) copy-start(bf16[32,64,128]{2,1,0:T(8,128)(2,1)} %own.1) | copy-start | bytes 1572868
  1.9 46.2 %copy-start.2 = (bf16[128,128]{1,0:T(8,128)(2,1)S(1)}, bf16[128,128]{1,0:T(8,128)(2,1)}, u32[]{:S(2)}) copy-start(bf16[128,128]{1,0:T(8,128)(2,1)} %cmap.1) | copy-start | bytes 98308
  1.9 46.2 %copy-start.3 = (bf16[32,128,128]{2,1,0:T(8,128)(2,1)S(1)}, bf16[32,128,128]{2,1,0:T(8,128)(2,1)}, u32[]{:S(2)}) copy-start(bf16[32,128,128]{2,1,0:T(8,128)(2,1)} %binv.1) | copy-start | bytes 3145732
  1.9 46.2 %copy-start.6 = (bf16[128,128]{1,0:T(8,128)(2,1)S(1)}, bf16[128,128]{1,0:T(8,128)(2,1)}, u32[]{:S(2)}) copy-start(bf16[128,128]{1,0:T(8,128)(2,1)} %pot.1) | copy-start | bytes 98308
  2.9 10.6 %collective-permute-start.7 = (f32[32,128]{1,0:T(8,128)S(1)}, f32[32,128]{1,0:T(8,128)S(1)}, u32[]{:S(2)}, u32[]{:S(2)}) collective-permute-start(f32[32,128]{1,0:T(8,128)S(1)} %fusion.6), channel_id=1, source_target_pairs={{0,24},{1,25},{2,26},{3,27},{4,28},{5,29},{6,30},{7,31}} | collective-permute-start | bytes 49160 | tf_op jit(solution)/shard_map/ppermute | solution.py:96
  3.6 11.9 %collective-permute-start.6 = (f32[32,128]{1,0:T(8,128)S(1)}, f32[32,128]{1,0:T(8,128)S(1)}, u32[]{:S(2)}, u32[]{:S(2)}) collective-permute-start(f32[32,128]{1,0:T(8,128)S(1)} %fusion.6), channel_id=1, source_target_pairs={{0,16},{1,17},{2,18},{3,19},{4,20},{5,21},{6,22},{7,23},{8,24},{9,... | collective-permute-start | bytes 49160 | tf_op jit(solution)/shard_map/ppermute | solution.py:96
  4.9 10.6 %collective-permute-start.5 = (f32[32,128]{1,0:T(8,128)S(1)}, f32[32,128]{1,0:T(8,128)S(1)}, u32[]{:S(2)}, u32[]{:S(2)}) collective-permute-start(f32[32,128]{1,0:T(8,128)S(1)} %fusion.6), channel_id=1, source_target_pairs={{0,8},{1,9},{2,10},{3,11},{4,12},{5,13},{6,14},{7,15},{8,16},{9,17... | collective-permute-start | bytes 49160 | tf_op jit(solution)/shard_map/ppermute | solution.py:96
  8.7 22.9 %collective-permute-start.4 = (bf16[32,64,128]{2,1,0:T(8,128)(2,1)}, bf16[32,64,128]{2,1,0:T(8,128)(2,1)S(1)}, u32[]{:S(2)}, u32[]{:S(2)}) collective-permute-start(bf16[32,64,128]{2,1,0:T(8,128)(2,1)} %own.1), channel_id=1, source_target_pairs={{0,15},{1,8},{2,9},{3,10},{4,11},{5,12},{6,13},{7,14},{8,23},{9,16... | collective-permute-start | bytes 1572872 | tf_op jit(solution)/shard_map/ppermute | solution.py:96
  10.6 21.5 %collective-permute-start.3 = (bf16[32,64,128]{2,1,0:T(8,128)(2,1)}, bf16[32,64,128]{2,1,0:T(8,128)(2,1)}, u32[]{:S(2)}, u32[]{:S(2)}) collective-permute-start(bf16[32,64,128]{2,1,0:T(8,128)(2,1)} %own.1), channel_id=1, source_target_pairs={{0,7},{1,0},{2,1},{3,2},{4,3},{5,4},{6,5},{7,6},{8,15},{9,8},{10,9... | collective-permute-start | bytes 1572872 | tf_op jit(solution)/shard_map/ppermute | solution.py:96
  13.5 25.2 %collective-permute-start.2 = (bf16[32,64,128]{2,1,0:T(8,128)(2,1)}, bf16[32,64,128]{2,1,0:T(8,128)(2,1)}, u32[]{:S(2)}, u32[]{:S(2)}) collective-permute-start(bf16[32,64,128]{2,1,0:T(8,128)(2,1)} %own.1), channel_id=1, source_target_pairs={{0,9},{1,10},{2,11},{3,12},{4,13},{5,14},{6,15},{7,8},{8,17},{9,18... | collective-permute-start | bytes 1572872 | tf_op jit(solution)/shard_map/ppermute | solution.py:96
  15.5 23.2 %collective-permute-start.1 = (bf16[32,64,128]{2,1,0:T(8,128)(2,1)}, bf16[32,64,128]{2,1,0:T(8,128)(2,1)}, u32[]{:S(2)}, u32[]{:S(2)}) collective-permute-start(bf16[32,64,128]{2,1,0:T(8,128)(2,1)} %own.1), channel_id=1, source_target_pairs={{0,1},{1,2},{2,3},{3,4},{4,5},{5,6},{6,7},{7,0},{8,9},{9,10},{10,1... | collective-permute-start | bytes 1572872 | tf_op jit(solution)/shard_map/ppermute | solution.py:96
  15.6 32.5 %collective-permute-start = (bf16[32,64,128]{2,1,0:T(8,128)(2,1)}, bf16[32,64,128]{2,1,0:T(8,128)(2,1)}, u32[]{:S(2)}, u32[]{:S(2)}) collective-permute-start(bf16[32,64,128]{2,1,0:T(8,128)(2,1)} %own.1), channel_id=1, source_target_pairs={{0,8},{1,9},{2,10},{3,11},{4,12},{5,13},{6,14},{7,15},{8,16},{9,17... | collective-permute-start | bytes 1572872 | tf_op jit(solution)/shard_map/ppermute | solution.py:96
  48.1 1.2 %copy-start.4 = (bf16[30,128,128]{2,1,0:T(8,128)(2,1)S(1)}, bf16[30,128,128]{2,1,0:T(8,128)(2,1)}, u32[]{:S(2)}) copy-start(bf16[30,128,128]{2,1,0:T(8,128)(2,1)} %param.12) | copy-start | bytes 2949124

commit v2 on v1

--- a/solution.py
+++ b/solution.py
@@ -1,3 +1,5 @@
+import functools
+
 import jax
 import jax.numpy as jnp
 from jax import lax
@@ -6,10 +8,162 @@
 from jax.sharding import PartitionSpec as P
 
 GROUP = 4
+PIECES = 4
+MESH = pl.DeviceIdType.MESH
+LEFT, RIGHT, PREV, LEFT_PREV, RIGHT_PREV = range(5)
+
+
+def halo_kernel(
+    n_tm, n_clus, own_hbm, own, cmap, profile, halo, toep, before, totals,
+    send, sib_sem, edge_sem, prev_sem, sib_prev_sem, edge_prev_sem, total_send, total_recv,
+):
+    i, c = lax.axis_index("tm"), lax.axis_index("clus")
+    per_dev, steps, unknowns = own.shape
+    slots, _, window = toep.shape
+    core = lax.rem(c, 2)
+    sibling = c + 1 - 2 * core
+    beyond = lax.rem(c + 2 * core - 1 + n_clus, n_clus)
+    sib_slot, beyond_slot = 1 - core, core
+    wraps = (c == 0) | (c == n_clus - 1)
+    piece = per_dev // PIECES
+
+    barrier = pltpu.get_barrier_semaphore()
+    for other in (sibling, beyond):
+        pl.semaphore_signal(barrier, inc=1, device_id=(i, other), device_id_type=MESH)
+    for by in range(1, n_tm):
+        pl.semaphore_signal(
+            barrier, inc=1, device_id=(lax.rem(i + by, n_tm), c), device_id_type=MESH
+        )
+    pl.semaphore_wait(barrier, n_tm + 1)
+
+    def remote(src, dst, sent, received, tm, clus):
+        return pltpu.make_async_remote_copy(
+            src_ref=src, dst_ref=dst, send_sem=sent, recv_sem=received,
+            device_id=(tm, clus), device_id_type=MESH,
+        )
+
+    later = lax.rem(i + 1, n_tm)
+
+    def rows(j):
+        return pl.ds(j * piece, piece)
+
+    def to_edge(j):
+        return remote(
+            own_hbm.at[rows(j)], halo.at[sib_slot, rows(j)], send.at[0, j], edge_sem.at[j],
+            i, beyond,
+        )
+
+    def to_later(j):
+        return remote(
+            own_hbm.at[rows(j)], halo.at[PREV, rows(j)], send.at[1, j], prev_sem.at[j], later, c
+        )
+
+    def prev_to_sib(j):
+        return remote(
+            halo.at[PREV, rows(j)], halo.at[beyond_slot + 3, rows(j)], send.at[2, j],
+            sib_prev_sem.at[j], i, sibling,
+        )
+
+    def prev_to_edge(j):
+        return remote(
+            halo.at[PREV, rows(j)], halo.at[sib_slot + 3, rows(j)], send.at[3, j],
+            edge_prev_sem.at[j], i, beyond,
+        )
+
+    def edge_to_later(j):
+        return remote(
+            halo.at[beyond_slot, rows(j)], halo.at[beyond_slot + 3, rows(j)], send.at[4, j],
+            edge_prev_sem.at[j], later, c,
+        )
+
+    to_sib = remote(
+        own_hbm, halo.at[beyond_slot], send.at[5, 0], sib_sem.at[0], i, sibling
+    )
+    has_prev, has_later = i > 0, i < n_tm - 1
+    for j in range(PIECES):
+        to_edge(j).start()
+
+        @pl.when(has_later)
+        def _():
+            to_later(j).start()
+
+    to_sib.start()
+
+    sums = jnp.sum(own[...].astype(jnp.float32), axis=1)
+    totals[n_tm] = jnp.dot(
+        sums, cmap[...].astype(jnp.float32), precision=lax.Precision.HIGHEST,
+        preferred_element_type=jnp.float32,
+    )
+
+    def total_to(by):
+        return remote(
+            totals.at[n_tm], totals.at[by], total_send.at[by], total_recv.at[by],
+            lax.rem(i + by, n_tm), c,
+        )
+
+    for by in range(1, n_tm):
+
+        @pl.when(i + by < n_tm)
+        def _():
+            total_to(by).start()
+
+    for k in range(slots):
+        line = jnp.broadcast_to(profile[pl.ds(k, 1)].astype(jnp.float32), (steps, window))
+        toep[k] = pltpu.roll(line, 0, 1, stride=1, stride_axis=0).astype(toep.dtype)
+
+    for j in range(PIECES):
+
+        @pl.when(has_prev)
+        def _():
+            to_later(j).wait_recv()
+            prev_to_sib(j).start()
+
+            @pl.when(jnp.logical_not(wraps))
+            def _():
+                prev_to_edge(j).start()
+
+        to_edge(j).wait_recv()
+
+        @pl.when(wraps & has_later)
+        def _():
+            edge_to_later(j).start()
+
+    before[...] = jnp.zeros(before.shape, before.dtype)
+    for by in range(1, n_tm):
+
+        @pl.when(i >= by)
+        def _():
+            total_to(by).wait_recv()
+            before[...] += totals[by]
+
+        @pl.when(i + by < n_tm)
+        def _():
+            total_to(by).wait_send()
+
+    to_sib.wait()
+    for j in range(PIECES):
+        to_edge(j).wait_send()
+
+        @pl.when(has_later)
+        def _():
+            to_later(j).wait_send()
+
+        @pl.when(has_prev)
+        def _():
+            prev_to_sib(j).wait()
+            prev_to_edge(j).wait_recv()
+
+        @pl.when(has_prev & jnp.logical_not(wraps))
+        def _():
+            prev_to_edge(j).wait_send()
+
+        @pl.when(wraps & has_later)
+        def _():
+            edge_to_later(j).wait_send()
 
 
 def sweep_kernel(
-    ids, own, prev, left, left_prev, right, right_prev, exc, toep, coup, binv, cmap, pot, before,
+    ids, early, own, halo, exc, toep, coup, binv, cmap, pot, before,
     upd, res, ext, filt, lower, sems,
 ):
     group = pl.program_id(0)
@@ -19,17 +173,30 @@
 
     @pl.when(group == 0)
     def _():
-        copies = []
-        for n, (old, new) in enumerate(((left_prev, left), (prev, own), (right_prev, right))):
-            rows = pl.ds(n * per_dev, per_dev)
+        sides = ((LEFT_PREV, halo.at[LEFT]), (PREV, own), (RIGHT_PREV, halo.at[RIGHT]))
+        copies, old_copies = [], []
+        for n, (old, new) in enumerate(sides):
+            place = pl.ds(n * per_dev, per_dev)
             copies.append(
-                pltpu.make_async_copy(old, ext.at[rows, pl.ds(0, lags)], sems.at[2 * n])
+                pltpu.make_async_copy(new, ext.at[place, pl.ds(lags, steps)], sems.at[2 * n])
             )
-            copies.append(
-                pltpu.make_async_copy(new, ext.at[rows, pl.ds(lags, steps)], sems.at[2 * n + 1])
+            old_copies.append(
+                pltpu.make_async_copy(
+                    halo.at[old], ext.at[place, pl.ds(0, lags)], sems.at[2 * n + 1]
+                )
             )
         for copy in copies:
             copy.start()
+
+        @pl.when(early[0] == 0)
+        def _():
+            for copy in old_copies:
+                copy.start()
+
+        @pl.when(early[0] != 0)
+        def _():
+            ext[:, pl.ds(0, lags)] = jnp.zeros((ext.shape[0], lags, unknowns), ext.dtype)
+
         ext[3 * per_dev] = jnp.zeros((window, unknowns), ext.dtype)
         size = GROUP * steps
         row = lax.broadcasted_iota(jnp.int32, (size, size), 0)
@@ -38,6 +205,11 @@
         lower[...] = jnp.where(keep, 1.0, 0.0).astype(lower.dtype)
         for copy in copies:
             copy.wait()
+
+        @pl.when(early[0] == 0)
+        def _():
+            for copy in old_copies:
+                copy.wait()
 
     first = group * GROUP
     for k in range(slots):
@@ -87,53 +259,52 @@
     n_tm, n_clus = lax.axis_size("tm"), lax.axis_size("clus")
     total = per_dev * n_clus
 
-    def sent(x, by_tm, by_clus):
-        pairs = [
-            (t * n_clus + c, (t + by_tm) * n_clus + (c + by_clus) % n_clus)
-            for t in range(n_tm - by_tm)
-            for c in range(n_clus)
-        ]
-        return lax.ppermute(x, ("tm", "clus"), pairs)
-
-    left = sent(currents, 0, 1)
-    right = sent(currents, 0, -1)
-    left_prev = sent(currents, 1, 1)
-    right_prev = sent(currents, 1, -1)
-    prev = sent(currents, 1, 0)
-
-    totals = jnp.dot(
-        jnp.sum(currents.astype(jnp.float32), axis=1),
-        charge_map.astype(jnp.float32),
-        precision=lax.Precision.HIGHEST,
-    )
-    before = jnp.zeros_like(totals)
-    for by in range(1, n_tm):
-        before = before + sent(totals, by, 0)
+    vmem = pl.BlockSpec(memory_space=pltpu.VMEM)
+    anywhere = pl.BlockSpec(memory_space=pl.ANY)
+    profile = jnp.pad(lag_profile[:, ::-1], ((0, 0), (1, window - lags - 1)))
+    halo, toep, before = pl.pallas_call(
+        functools.partial(halo_kernel, n_tm, n_clus),
+        in_specs=[anywhere, vmem, vmem, vmem],
+        out_specs=[anywhere, vmem, vmem],
+        out_shape=[
+            jax.ShapeDtypeStruct((5,) + currents.shape, jnp.bfloat16),
+            jax.ShapeDtypeStruct((slots, steps, window), jnp.bfloat16),
+            jax.ShapeDtypeStruct((per_dev, patches), jnp.float32),
+        ],
+        scratch_shapes=[
+            pltpu.VMEM((n_tm + 1, per_dev, patches), jnp.float32),
+            pltpu.SemaphoreType.DMA((6, PIECES)),
+            pltpu.SemaphoreType.DMA((1,)),
+            pltpu.SemaphoreType.DMA((PIECES,)),
+            pltpu.SemaphoreType.DMA((PIECES,)),
+            pltpu.SemaphoreType.DMA((PIECES,)),
+            pltpu.SemaphoreType.DMA((PIECES,)),
+            pltpu.SemaphoreType.DMA((n_tm,)),
+            pltpu.SemaphoreType.DMA((n_tm,)),
+        ],
+        compiler_params=pltpu.CompilerParams(
+            collective_id=0, has_side_effects=True, vmem_limit_bytes=32 << 20
+        ),
+    )(currents, currents, charge_map, profile)
 
     first_local = (lax.axis_index("clus") - 1) * per_dev
     ids = jnp.where(neighbours >= 0, (neighbours - first_local) % total, 3 * per_dev)
-    lag_index = jnp.arange(steps)[:, None] + lags - jnp.arange(window)[None, :]
-    onehot = (lag_index[:, :, None] == jnp.arange(lags)[None, None, :]).astype(jnp.bfloat16)
-    toep = jnp.einsum(
-        "kl,tsl->kts", lag_profile, onehot, preferred_element_type=jnp.float32
-    ).astype(jnp.bfloat16)
-
-    anywhere = pl.BlockSpec(memory_space=pl.ANY)
+    early = (lax.axis_index("tm") == 0).astype(jnp.int32).reshape(1)
 
     def whole(*shape):
-        return pl.BlockSpec(shape, lambda g, ids: (0,) * len(shape))
+        return pl.BlockSpec(shape, lambda g, ids, early: (0,) * len(shape))
 
     def grouped(*shape):
-        return pl.BlockSpec((GROUP,) + shape, lambda g, ids: (g,) + (0,) * len(shape))
+        return pl.BlockSpec((GROUP,) + shape, lambda g, ids, early: (g,) + (0,) * len(shape))
 
     size = GROUP * steps
     pairs = per_dev * slots * steps * unknowns
     return pl.pallas_call(
         sweep_kernel,
         grid_spec=pltpu.PrefetchScalarGridSpec(
-            num_scalar_prefetch=1,
+            num_scalar_prefetch=2,
             grid=(per_dev // GROUP,),
-            in_specs=[anywhere] * 6
+            in_specs=[anywhere] * 2
             + [
                 grouped(steps, unknowns),
                 whole(slots, steps, window),
@@ -141,7 +312,7 @@
                 grouped(unknowns, unknowns),
                 whole(unknowns, patches),
                 whole(patches, unknowns),
-                pl.BlockSpec((None, GROUP, patches), lambda g, ids: (g, 0, 0)),
+                pl.BlockSpec((None, GROUP, patches), lambda g, ids, early: (g, 0, 0)),
             ],
             out_specs=[grouped(steps, unknowns), grouped(steps, unknowns)],
             scratch_shapes=[
@@ -160,7 +331,7 @@
             flops=2 * pairs * (window + unknowns), bytes_accessed=8 << 20, transcendentals=0
         ),
     )(
-        ids, currents, prev, left, left_prev, right, right_prev, excitation, toep,
+        ids, early, currents, halo, excitation, toep,
         couplings.reshape(slots * unknowns, unknowns), block_inverses, charge_map, potential,
         before.reshape(per_dev // GROUP, GROUP, patches),
     )

time: 67 us -> 47.9 us (0.71); the launches traced: 65.7 us -> 47.3 us
  waiting for transfers between devices: 28.1 us -> 0 us
  Pallas kernels: 16.4 us -> 37.2 us
  starting transfers between devices: 14.4 us -> 0 us
  local copies, waits for them, and re-layouts: 2.47 us -> 8.67 us
  matrix products: 2.24 us -> 0 us
    ppermute x8 -> x0, waiting for transfers between devices: 28.1 us -> none  [sent(): return lax.ppermute(x, ('tm', 'clus'), pairs)]
    pallas_call x0 -> x1, Pallas kernels: none -> 22.1 us  [on_device(): pl.pallas_call(functools.partial(halo_kernel, n_tm, n_clus), in_specs=[an...]
    ppermute x8 -> x0, starting transfers between devices: 14.4 us -> none  [sent(): return lax.ppermute(x, ('tm', 'clus'), pairs)]
    unnamed x16, local copies, waits for them, and re-layouts: 1.24 us -> 7.81 us
    dot_general x2 -> x0, matrix products: 2.24 us -> none  [the longest x1 1.25 us: on_device(): jnp.einsum('kl,tsl->kts', lag_profile, onehot, preferred_element_type=jnp...]
    pallas_call x1, Pallas kernels: 16.4 us -> 15.1 us  [on_device(): pl.pallas_call(sweep_kernel, grid_spec=pltpu.PrefetchScalarGridSpec(num_s...]
    dot_general x1 -> x0, local copies, waits for them, and re-layouts: 1.23 us -> none  [on_device(): jnp.einsum('kl,tsl->kts', lag_profile, onehot, preferred_element_type=jnp...]
    reduce_sum x1 -> x0, other arithmetic: 1.21 us -> none  [on_device(): jnp.sum(currents.astype(jnp.float32), axis=1)]
  transfers between devices with their start and end apart: 8 -> 0, of which waited for: 4 -> 0; matrix products, arithmetic and copies ran while one was open for 4% -> 0% of each run, Pallas kernels for 0% -> 0%
where the time goes in v2:
time: 47.9 us; the launch traced here: 47.3 us
  Pallas kernels  37.2 us (78%)
  local copies, waits for them, and re-layouts  8.67 us (18%)
  other arithmetic  0.73 us (2%)
  between operations  0.67 us (1%)
    pallas_call x1, Pallas kernels, on_device(): pl.pallas_call(functools.partial(halo_kernel, n_tm, n_clus), in_specs=[an...  22.1 us
    pallas_call x1, Pallas kernels, on_device(): pl.pallas_call(sweep_kernel, grid_spec=pltpu.PrefetchScalarGridSpec(num_s...  15.1 us
    unnamed x16, local copies, waits for them, and re-layouts  7.81 us

profile of v2, /device:TPU:5, one launch (start us, length us, event | category | flops | bytes accessed | tf_op | source)
XLA Modules:
  0.0 47.3 jit_solution(9693451477925392136)
XLA Ops:
  0.6 0.8 %rev.3 = bf16[30,64]{1,0:T(8,128)(2,1)S(1)} reverse(bf16[30,64]{1,0:T(8,128)(2,1)} %param.11), dimensions={1} | reverse | bytes 7680 | tf_op jit(solution)/shard_map/rev | solution.py:264
  1.4 0.1 pad.4.profile
  1.5 0.7 %fusion.1.ids = s32[32,30]{1,0:T(8,128)S(1)} fusion(s32[32,30]{1,0:T(8,128)} %param.10, s32[]{:T(128)S(6)} %mul.3), kind=kLoop, calls=%fused_computation.4 | loop fusion | flops 13440 | bytes 7684 | tf_op jit(solution)/shard_map/jit(_where)/select_n | solution.py:291
  2.2 0.0 copy-start
  2.2 1.0 %copy-done = bf16[32,64,128]{2,1,0:T(8,128)(2,1)S(1)} copy-done((bf16[32,64,128]{2,1,0:T(8,128)(2,1)S(1)}, bf16[32,64,128]{2,1,0:T(8,128)(2,1)}, u32[]{:S(2)}) %copy-start) | copy-done | bytes 524312
  3.3 0.0 copy-start.2
  3.3 0.8 %copy-done.2 = bf16[128,128]{1,0:T(8,128)(2,1)S(1)} copy-done((bf16[128,128]{1,0:T(8,128)(2,1)S(1)}, bf16[128,128]{1,0:T(8,128)(2,1)}, u32[]{:S(2)}) %copy-start.2) | copy-done | bytes 32792
  4.0 22.1 %shard_map.95 = (bf16[5,32,64,128]{3,2,1,0:T(8,128)(2,1)S(1)}, bf16[30,64,128]{2,1,0:T(8,128)(2,1)S(1)}, f32[32,128]{1,0:T(8,128)S(1)}) custom-call(bf16[32,64,128]{2,1,0:T(8,128)(2,1)S(1)} %copy-done, bf16[32,64,128]{2,1,0:T(8,128)(2,1)S(1)} %copy-done, bf16[128,128]{1,0:T(8,128)(2,1)S(1)} %copy-done.2, bf16[30,128]{1,0:T(8,128)(2,1)S(1)} %pad.4.profile), custom_call_target="tpu_custom_call" | custom-call | tf_op jit(solution)/shard_map/pallas_call | solution.py:265
  26.1 0.0 copy-start.1
  26.1 1.0 %copy-done.1 = bf16[32,64,128]{2,1,0:T(8,128)(2,1)S(1)} copy-done((bf16[32,64,128]{2,1,0:T(8,128)(2,1)S(1)}, bf16[32,64,128]{2,1,0:T(8,128)(2,1)}, u32[]{:S(2)}) %copy-start.1) | copy-done | bytes 524312
  27.2 0.0 copy-start.3
  27.2 0.8 %copy-done.3 = bf16[128,128]{1,0:T(8,128)(2,1)S(1)} copy-done((bf16[128,128]{1,0:T(8,128)(2,1)S(1)}, bf16[128,128]{1,0:T(8,128)(2,1)}, u32[]{:S(2)}) %copy-start.3) | copy-done | bytes 32792
  27.9 0.0 copy-start.4
  27.9 1.2 %copy-done.4 = bf16[32,128,128]{2,1,0:T(8,128)(2,1)S(1)} copy-done((bf16[32,128,128]{2,1,0:T(8,128)(2,1)S(1)}, bf16[32,128,128]{2,1,0:T(8,128)(2,1)}, u32[]{:S(2)}) %copy-start.4) | copy-done | bytes 1048600
  29.1 0.0 copy-start.5
  29.1 1.2 %copy-done.5 = bf16[30,128,128]{2,1,0:T(8,128)(2,1)S(1)} copy-done((bf16[30,128,128]{2,1,0:T(8,128)(2,1)S(1)}, bf16[30,128,128]{2,1,0:T(8,128)(2,1)}, u32[]{:S(2)}) %copy-start.5) | copy-done | bytes 983064
  30.3 0.0 copy-start.6
  30.4 1.0 %copy-done.6 = bf16[32,64,128]{2,1,0:T(8,128)(2,1)S(1)} copy-done((bf16[32,64,128]{2,1,0:T(8,128)(2,1)S(1)}, bf16[32,64,128]{2,1,0:T(8,128)(2,1)}, u32[]{:S(2)}) %copy-start.6) | copy-done | bytes 524312
  31.4 0.0 copy-start.7
  31.4 0.8 %copy-done.7 = bf16[128,128]{1,0:T(8,128)(2,1)S(1)} copy-done((bf16[128,128]{1,0:T(8,128)(2,1)S(1)}, bf16[128,128]{1,0:T(8,128)(2,1)}, u32[]{:S(2)}) %copy-start.7) | copy-done | bytes 32792
  32.1 15.1 %shard_map.96 = (bf16[32,64,128]{2,1,0:T(8,128)(2,1)}, f32[32,64,128]{2,1,0:T(8,128)}) custom-call(s32[32,30]{1,0:T(8,128)S(1)} %fusion.1.ids, s32[1]{0:T(128)} %bitcast.early, bf16[32,64,128]{2,1,0:T(8,128)(2,1)S(1)} %copy-done.1, bf16[5,32,64,128]{3,2,1,0:T(8,128)(2,1)S(1)} %get-tuple-element.5.halo, bf16[32,64,128]{2,1,0:T(8,128)(2,1)S(1)} %copy-done.6, ...), custom_call_target="tpu_custom_call" | custom-call | flops 4026531840 | bytes 8388608 | tf_op jit(solution)/shard_map/pallas_call | solution.py:302
Async XLA Ops:
  2.2 1.0 %copy-start = (bf16[32,64,128]{2,1,0:T(8,128)(2,1)S(1)}, bf16[32,64,128]{2,1,0:T(8,128)(2,1)}, u32[]{:S(2)}) copy-start(bf16[32,64,128]{2,1,0:T(8,128)(2,1)} %own.3) | copy-start | bytes 1572868
  3.3 0.8 %copy-start.2 = (bf16[128,128]{1,0:T(8,128)(2,1)S(1)}, bf16[128,128]{1,0:T(8,128)(2,1)}, u32[]{:S(2)}) copy-start(bf16[128,128]{1,0:T(8,128)(2,1)} %cmap.3) | copy-start | bytes 98308
  26.1 1.0 %copy-start.1 = (bf16[32,64,128]{2,1,0:T(8,128)(2,1)S(1)}, bf16[32,64,128]{2,1,0:T(8,128)(2,1)}, u32[]{:S(2)}) copy-start(bf16[32,64,128]{2,1,0:T(8,128)(2,1)} %own.3) | copy-start | bytes 1572868
  27.2 0.8 %copy-start.3 = (bf16[128,128]{1,0:T(8,128)(2,1)S(1)}, bf16[128,128]{1,0:T(8,128)(2,1)}, u32[]{:S(2)}) copy-start(bf16[128,128]{1,0:T(8,128)(2,1)} %cmap.3) | copy-start | bytes 98308
  27.9 1.2 %copy-start.4 = (bf16[32,128,128]{2,1,0:T(8,128)(2,1)S(1)}, bf16[32,128,128]{2,1,0:T(8,128)(2,1)}, u32[]{:S(2)}) copy-start(bf16[32,128,128]{2,1,0:T(8,128)(2,1)} %binv.1) | copy-start | bytes 3145732
  29.1 1.2 %copy-start.5 = (bf16[30,128,128]{2,1,0:T(8,128)(2,1)S(1)}, bf16[30,128,128]{2,1,0:T(8,128)(2,1)}, u32[]{:S(2)}) copy-start(bf16[30,128,128]{2,1,0:T(8,128)(2,1)} %param.12) | copy-start | bytes 2949124
  30.3 1.0 %copy-start.6 = (bf16[32,64,128]{2,1,0:T(8,128)(2,1)S(1)}, bf16[32,64,128]{2,1,0:T(8,128)(2,1)}, u32[]{:S(2)}) copy-start(bf16[32,64,128]{2,1,0:T(8,128)(2,1)} %exc.1) | copy-start | bytes 1572868
  31.4 0.8 %copy-start.7 = (bf16[128,128]{1,0:T(8,128)(2,1)S(1)}, bf16[128,128]{1,0:T(8,128)(2,1)}, u32[]{:S(2)}) copy-start(bf16[128,128]{1,0:T(8,128)(2,1)} %pot.1) | copy-start | bytes 98308

commit v3 on v2

--- a/solution.py
+++ b/solution.py
@@ -8,13 +8,13 @@
 from jax.sharding import PartitionSpec as P
 
 GROUP = 4
-PIECES = 4
+PIECES = 8
 MESH = pl.DeviceIdType.MESH
 LEFT, RIGHT, PREV, LEFT_PREV, RIGHT_PREV = range(5)
 
 
 def halo_kernel(
-    n_tm, n_clus, own_hbm, own, cmap, profile, halo, toep, before, totals,
+    n_tm, n_clus, own_hbm, own, cmap, profile, coup, halo, toep, coup_t, before, totals,
     send, sib_sem, edge_sem, prev_sem, sib_prev_sem, edge_prev_sem, total_send, total_recv,
 ):
     i, c = lax.axis_index("tm"), lax.axis_index("clus")
@@ -107,9 +107,15 @@
         def _():
             total_to(by).start()
 
+    lags = profile.shape[1]
+    lag = lax.broadcasted_iota(jnp.int32, (lags, window), 0)
+    place = lax.broadcasted_iota(jnp.int32, (lags, window), 1)
+    turn = jnp.where(lag + place == lags, 1.0, 0.0).astype(jnp.bfloat16)
+    turned = jnp.dot(profile[...], turn, preferred_element_type=jnp.float32)
     for k in range(slots):
-        line = jnp.broadcast_to(profile[pl.ds(k, 1)].astype(jnp.float32), (steps, window))
+        line = jnp.broadcast_to(turned[k : k + 1], (steps, window))
         toep[k] = pltpu.roll(line, 0, 1, stride=1, stride_axis=0).astype(toep.dtype)
+        coup_t[:, pl.ds(k * unknowns, unknowns)] = coup[k].T
 
     for j in range(PIECES):
 
@@ -118,11 +124,11 @@
             to_later(j).wait_recv()
             prev_to_sib(j).start()
 
-            @pl.when(jnp.logical_not(wraps))
-            def _():
-                prev_to_edge(j).start()
-
         to_edge(j).wait_recv()
+
+        @pl.when(has_prev & jnp.logical_not(wraps))
+        def _():
+            prev_to_edge(j).start()
 
         @pl.when(wraps & has_later)
         def _():
@@ -163,10 +169,21 @@
 
 
 def sweep_kernel(
-    ids, early, own, halo, exc, toep, coup, binv, cmap, pot, before,
+    n_clus, neighbours, own, halo, exc, toep, coup_t, binv, cmap, pot, before,
     upd, res, ext, filt, lower, sems,
 ):
     group = pl.program_id(0)
+    has_prev = lax.axis_index("tm") > 0
+    first_local = (lax.axis_index("clus") - 1) * own.shape[0]
+    total = n_clus * own.shape[0]
+
+    def place_of(cluster, slot):
+        at = neighbours[cluster, slot]
+        to = at - first_local
+        to = jnp.where(to < 0, to + total, to)
+        to = jnp.where(to >= total, to - total, to)
+        return jnp.where(at < 0, 3 * own.shape[0], to)
+
     per_dev, steps, unknowns = own.shape
     slots, _, window = toep.shape
     lags = window - steps
@@ -188,12 +205,12 @@
         for copy in copies:
             copy.start()
 
-        @pl.when(early[0] == 0)
+        @pl.when(has_prev)
         def _():
             for copy in old_copies:
                 copy.start()
 
-        @pl.when(early[0] != 0)
+        @pl.when(jnp.logical_not(has_prev))
         def _():
             ext[:, pl.ds(0, lags)] = jnp.zeros((ext.shape[0], lags, unknowns), ext.dtype)
 
@@ -206,7 +223,7 @@
         for copy in copies:
             copy.wait()
 
-        @pl.when(early[0] == 0)
+        @pl.when(has_prev)
         def _():
             for copy in old_copies:
                 copy.wait()
@@ -214,15 +231,17 @@
     first = group * GROUP
     for k in range(slots):
         for c in range(0, GROUP, 2):
-            one = ext[ids[first + c, k]]
-            two = ext[ids[first + c + 1, k]]
+            one = ext[place_of(first + c, k)]
+            two = ext[place_of(first + c + 1, k)]
             both = jnp.concatenate([one, two], axis=1)
             out = jnp.dot(toep[k], both, preferred_element_type=jnp.float32)
             out = out.astype(jnp.bfloat16)
             lanes = pl.ds(k * unknowns, unknowns)
             filt[pl.ds(c * steps, steps), lanes] = out[:, :unknowns]
             filt[pl.ds((c + 1) * steps, steps), lanes] = out[:, unknowns:]
-    near = jnp.dot(filt[...], coup[...], preferred_element_type=jnp.float32)
+    near = lax.dot_general(
+        coup_t[...], filt[...], (((1,), (1,)), ((), ())), preferred_element_type=jnp.float32
+    ).T
 
     own_rows = ext[pl.ds(per_dev + first, GROUP), pl.ds(lags, steps)]
     own_rows = own_rows.reshape(GROUP * steps, unknowns)
@@ -234,7 +253,7 @@
     )
     patches = incr.shape[1]
     running = (sums[:, :patches] + sums[:, patches:]).reshape(GROUP, steps, patches)
-    charge = (running + before[...][:, None, :]).astype(jnp.bfloat16)
+    charge = (running + before[pl.ds(first, GROUP)][:, None, :]).astype(jnp.bfloat16)
     field = jnp.dot(
         charge.reshape(GROUP * steps, patches), pot[...], preferred_element_type=jnp.float32
     )
@@ -257,18 +276,17 @@
     window = steps + lags
     patches = charge_map.shape[1]
     n_tm, n_clus = lax.axis_size("tm"), lax.axis_size("clus")
-    total = per_dev * n_clus
 
     vmem = pl.BlockSpec(memory_space=pltpu.VMEM)
     anywhere = pl.BlockSpec(memory_space=pl.ANY)
-    profile = jnp.pad(lag_profile[:, ::-1], ((0, 0), (1, window - lags - 1)))
-    halo, toep, before = pl.pallas_call(
+    halo, toep, coup_t, before = pl.pallas_call(
         functools.partial(halo_kernel, n_tm, n_clus),
-        in_specs=[anywhere, vmem, vmem, vmem],
-        out_specs=[anywhere, vmem, vmem],
+        in_specs=[anywhere, vmem, vmem, vmem, vmem],
+        out_specs=[anywhere, vmem, vmem, vmem],
         out_shape=[
             jax.ShapeDtypeStruct((5,) + currents.shape, jnp.bfloat16),
             jax.ShapeDtypeStruct((slots, steps, window), jnp.bfloat16),
+            jax.ShapeDtypeStruct((unknowns, slots * unknowns), jnp.bfloat16),
             jax.ShapeDtypeStruct((per_dev, patches), jnp.float32),
         ],
         scratch_shapes=[
@@ -283,36 +301,32 @@
             pltpu.SemaphoreType.DMA((n_tm,)),
         ],
         compiler_params=pltpu.CompilerParams(
-            collective_id=0, has_side_effects=True, vmem_limit_bytes=32 << 20
+            collective_id=0, has_side_effects=True, vmem_limit_bytes=56 << 20
         ),
-    )(currents, currents, charge_map, profile)
-
-    first_local = (lax.axis_index("clus") - 1) * per_dev
-    ids = jnp.where(neighbours >= 0, (neighbours - first_local) % total, 3 * per_dev)
-    early = (lax.axis_index("tm") == 0).astype(jnp.int32).reshape(1)
+    )(currents, currents, charge_map, lag_profile, couplings)
 
     def whole(*shape):
-        return pl.BlockSpec(shape, lambda g, ids, early: (0,) * len(shape))
+        return pl.BlockSpec(shape, lambda g, ids: (0,) * len(shape))
 
     def grouped(*shape):
-        return pl.BlockSpec((GROUP,) + shape, lambda g, ids, early: (g,) + (0,) * len(shape))
+        return pl.BlockSpec((GROUP,) + shape, lambda g, ids: (g,) + (0,) * len(shape))
 
     size = GROUP * steps
     pairs = per_dev * slots * steps * unknowns
     return pl.pallas_call(
-        sweep_kernel,
+        functools.partial(sweep_kernel, n_clus),
         grid_spec=pltpu.PrefetchScalarGridSpec(
-            num_scalar_prefetch=2,
+            num_scalar_prefetch=1,
             grid=(per_dev // GROUP,),
             in_specs=[anywhere] * 2
             + [
                 grouped(steps, unknowns),
                 whole(slots, steps, window),
-                whole(slots * unknowns, unknowns),
+                whole(unknowns, slots * unknowns),
                 grouped(unknowns, unknowns),
                 whole(unknowns, patches),
                 whole(patches, unknowns),
-                pl.BlockSpec((None, GROUP, patches), lambda g, ids, early: (g, 0, 0)),
+                whole(per_dev, patches),
             ],
             out_specs=[grouped(steps, unknowns), grouped(steps, unknowns)],
             scratch_shapes=[
@@ -326,14 +340,14 @@
             jax.ShapeDtypeStruct(currents.shape, jnp.bfloat16),
             jax.ShapeDtypeStruct(currents.shape, jnp.float32),
         ],
-        compiler_params=pltpu.CompilerParams(vmem_limit_bytes=40 << 20),
+        compiler_params=pltpu.CompilerParams(vmem_limit_bytes=56 << 20),
         cost_estimate=pl.CostEstimate(
             flops=2 * pairs * (window + unknowns), bytes_accessed=8 << 20, transcendentals=0
         ),
     )(
-        ids, early, currents, halo, excitation, toep,
-        couplings.reshape(slots * unknowns, unknowns), block_inverses, charge_map, potential,
-        before.reshape(per_dev // GROUP, GROUP, patches),
+        neighbours, currents, halo, excitation, toep,
+        coup_t, block_inverses, charge_map, potential,
+        before,
     )
 
 

time: 47.9 us -> 45.2 us (0.944)
  local copies, waits for them, and re-layouts: 8.67 us -> 0 us
  Pallas kernels: 37.2 us -> 44.3 us
  other arithmetic: 0.73 us -> 0 us
    unnamed x16 -> x0, local copies, waits for them, and re-layouts: 7.81 us -> none
    pallas_call x1, Pallas kernels: 15.1 us -> 19.1 us  [on_device(): pl.pallas_call(functools.partial(sweep_kernel, n_clus), grid_spec=pltpu.P...]
    pallas_call x1, Pallas kernels: 22.1 us -> 25.2 us  [on_device(): pl.pallas_call(functools.partial(halo_kernel, n_tm, n_clus), in_specs=[an...]
    rev x1 -> x0, local copies, waits for them, and re-layouts: 0.78 us -> none  [on_device(): profile = jnp.pad(lag_profile[:, ::-1], ((0, 0), (1, window - lags - 1)))]
    select_n x1 -> x0, other arithmetic: 0.73 us -> none  [on_device(): jnp.where(neighbours >= 0, (neighbours - first_local) % total, 3 * per_dev)]
where the time goes in v3:
time: 45.2 us; the launch traced here: 44.9 us
  Pallas kernels  44.3 us (98%)
  between operations  0.64 us (1%)
    pallas_call x1, Pallas kernels, on_device(): pl.pallas_call(functools.partial(halo_kernel, n_tm, n_clus), in_specs=[an...  25.2 us
    pallas_call x1, Pallas kernels, on_device(): pl.pallas_call(functools.partial(sweep_kernel, n_clus), grid_spec=pltpu.P...  19.1 us

profile of v3, /device:TPU:5, one launch (start us, length us, event | category | flops | bytes accessed | tf_op | source)
XLA Modules:
  0.0 44.9 jit_solution(16569721576770093039)
XLA Ops:
  0.6 25.2 %shard_map.95 = (bf16[5,32,64,128]{3,2,1,0:T(8,128)(2,1)}, bf16[30,64,128]{2,1,0:T(8,128)(2,1)}, bf16[128,3840]{1,0:T(8,128)(2,1)}, f32[32,128]{1,0:T(8,128)}) custom-call(bf16[32,64,128]{2,1,0:T(8,128)(2,1)} %own.3, bf16[32,64,128]{2,1,0:T(8,128)(2,1)} %own.3, bf16[128,128]{1,0:T(8,128)(2,1)} %cmap.3, bf16[30,64]{1,0:T(8,128)(2,1)} %profile.1, ...), custom_call_target="tpu_custom_call" | custom-call | tf_op jit(solution)/shard_map/pallas_call | solution.py:282
  25.8 19.1 %shard_map.96 = (bf16[32,64,128]{2,1,0:T(8,128)(2,1)}, f32[32,64,128]{2,1,0:T(8,128)}) custom-call(s32[32,30]{1,0:T(8,128)} %neighbours.1, bf16[32,64,128]{2,1,0:T(8,128)(2,1)} %own.3, bf16[5,32,64,128]{3,2,1,0:T(8,128)(2,1)} %get-tuple-element.6.halo, bf16[32,64,128]{2,1,0:T(8,128)(2,1)} %exc.1, bf16[30,64,128]{2,1,0:T(8,128)(2,1)} %get-tuple-element.7.toep, ...), custom_call_target="tpu_custom_call" | custom-call | flops 4026531840 | bytes 8388608 | tf_op jit(solution)/shard_map/pallas_call | solution.py:316

commit v4 on v3

v4 whole, which is shorter than its diff:
```python
import functools

import jax
import jax.numpy as jnp
from jax import lax
from jax.experimental import pallas as pl
from jax.experimental.pallas import tpu as pltpu
from jax.sharding import PartitionSpec as P

GROUP = 4
PIECES = 8
MESH = pl.DeviceIdType.MESH


def sweep_kernel(
    n_tm, n_clus, own_hbm, exc_hbm, coup_hbm, binv_hbm, neighbours, cmap, pot, profile,
    upd_hbm, res_hbm,
    ext, filt, toep, lower, coup, binv, exc, base, upd, res, before, totals,
    send, sib_sem, edge_sem, prev_sem, sib_prev_sem, edge_prev_sem, total_send, total_recv,
    load_sem, store_sem,
):
    i, c = lax.axis_index("tm"), lax.axis_index("clus")
    per_dev, steps, unknowns = own_hbm.shape
    slots, _, window = toep.shape
    lags = profile.shape[1]
    patches = cmap.shape[1]
    groups = per_dev // GROUP
    size = GROUP * steps
    core = lax.rem(c, 2)
    sibling = c + 1 - 2 * core
    beyond = lax.rem(c + 2 * core - 1 + n_clus, n_clus)
    wraps = (c == 0) | (c == n_clus - 1)
    has_prev, has_later = i > 0, i < n_tm - 1
    later = lax.rem(i + 1, n_tm)
    piece = per_dev // PIECES
    from_beyond, from_sibling = 2 * core, 2 - 2 * core

    barrier = pltpu.get_barrier_semaphore()
    for other in (sibling, beyond):
        pl.semaphore_signal(barrier, inc=1, device_id=(i, other), device_id_type=MESH)
    for by in range(1, n_tm):
        pl.semaphore_signal(
            barrier, inc=1, device_id=(lax.rem(i + by, n_tm), c), device_id_type=MESH
        )
    pl.semaphore_wait(barrier, n_tm + 1)

    def remote(src, dst, sent, received, tm, clus):
        return pltpu.make_async_remote_copy(
            src_ref=src, dst_ref=dst, send_sem=sent, recv_sem=received,
            device_id=(tm, clus), device_id_type=MESH,
        )

    def mine(j):
        return own_hbm.at[pl.ds(j * piece, piece)]

    def new(region, j):
        return ext.at[pl.ds(region * per_dev + j * piece, piece), pl.ds(lags, steps)]

    def old(region, j):
        return ext.at[pl.ds(region * per_dev + j * piece, piece), pl.ds(0, lags)]

    def to_edge(j):
        return remote(
            mine(j), new(from_sibling, j), send.at[0, j], edge_sem.at[j], i, beyond
        )

    def to_later(j):
        return remote(mine(j), old(1, j), send.at[1, j], prev_sem.at[j], later, c)

    def prev_to_sib(j):
        return remote(
            old(1, j), old(from_beyond, j), send.at[2, j], sib_prev_sem.at[j], i, sibling
        )

    def prev_to_edge(j):
        return remote(
            old(1, j), old(from_sibling, j), send.at[3, j], edge_prev_sem.at[j], i, beyond
        )

    def edge_to_later(j):
        return remote(
            new(from_beyond, j), old(from_beyond, j), send.at[4, j], edge_prev_sem.at[j],
            later, c,
        )

    to_sib = remote(
        own_hbm, ext.at[pl.ds(from_beyond * per_dev, per_dev), pl.ds(lags, steps)],
        send.at[5, 0], sib_sem.at[0], i, sibling,
    )
    for j in range(PIECES):
        to_edge(j).start()

        @pl.when(has_later)
        def _():
            to_later(j).start()

    to_sib.start()

    own_rows = (pl.ds(per_dev, per_dev), pl.ds(lags, steps))
    load_own = pltpu.make_async_copy(own_hbm, ext.at[own_rows], load_sem.at[0])
    loads = [
        pltpu.make_async_copy(exc_hbm, exc, load_sem.at[1]),
        pltpu.make_async_copy(coup_hbm, coup, load_sem.at[2]),
        pltpu.make_async_copy(binv_hbm, binv, load_sem.at[3]),
    ]
    load_own.start()
    for load in loads:
        load.start()

    ext[3 * per_dev] = jnp.zeros((window, unknowns), ext.dtype)

    @pl.when(jnp.logical_not(has_prev))
    def _():
        ext[pl.ds(0, 3 * per_dev), pl.ds(0, lags)] = jnp.zeros(
            (3 * per_dev, lags, unknowns), ext.dtype
        )

    load_own.wait()
    sums = jnp.sum(ext[own_rows].astype(jnp.float32), axis=1)
    totals[n_tm] = jnp.dot(
        sums, cmap[...].astype(jnp.float32), precision=lax.Precision.HIGHEST,
        preferred_element_type=jnp.float32,
    )

    def total_to(by):
        return remote(
            totals.at[n_tm], totals.at[by], total_send.at[by], total_recv.at[by],
            lax.rem(i + by, n_tm), c,
        )

    for by in range(1, n_tm):

        @pl.when(i + by < n_tm)
        def _():
            total_to(by).start()

    lag = lax.broadcasted_iota(jnp.int32, (lags, window), 0)
    place = lax.broadcasted_iota(jnp.int32, (lags, window), 1)
    turn = jnp.where(lag + place == lags, 1.0, 0.0).astype(jnp.bfloat16)
    turned = jnp.dot(profile[...], turn, preferred_element_type=jnp.float32)
    for k in range(slots):
        line = jnp.broadcast_to(turned[k : k + 1], (steps, window))
        toep[k] = pltpu.roll(line, 0, 1, stride=1, stride_axis=0).astype(toep.dtype)

    row = lax.broadcasted_iota(jnp.int32, (size, size), 0)
    col = lax.broadcasted_iota(jnp.int32, (size, size), 1)
    keep = (row >= col) & (row // steps == col // steps)
    lower[...] = jnp.where(keep, 1.0, 0.0).astype(lower.dtype)

    for j in range(PIECES):

        @pl.when(has_prev)
        def _():
            to_later(j).wait_recv()
            prev_to_sib(j).start()

        to_edge(j).wait_recv()

        @pl.when(has_prev & jnp.logical_not(wraps))
        def _():
            prev_to_edge(j).start()

        @pl.when(wraps & has_later)
        def _():
            edge_to_later(j).start()

    before[...] = jnp.zeros(before.shape, before.dtype)
    for by in range(1, n_tm):

        @pl.when(i >= by)
        def _():
            total_to(by).wait_recv()
            before[...] += totals[by]

    for load in loads:
        load.wait()

    def charge_group(group, carry):
        first = group * GROUP
        rows = ext[pl.ds(per_dev + first, GROUP), pl.ds(lags, steps)].reshape(size, unknowns)
        incr = jnp.dot(rows, cmap[...], preferred_element_type=jnp.float32)
        high = incr.astype(jnp.bfloat16)
        rest = (incr - high.astype(jnp.float32)).astype(jnp.bfloat16)
        sums = jnp.dot(
            lower[...], jnp.concatenate([high, rest], axis=1), preferred_element_type=jnp.float32
        )
        running = (sums[:, :patches] + sums[:, patches:]).reshape(GROUP, steps, patches)
        charge = (running + before[pl.ds(first, GROUP)][:, None, :]).astype(jnp.bfloat16)
        field = jnp.dot(
            charge.reshape(size, patches), pot[...], preferred_element_type=jnp.float32
        )
        field = field.reshape(GROUP, steps, unknowns)
        place = pl.ds(first, GROUP)
        base[place] = exc[place].astype(jnp.float32) - field
        return carry

    lax.fori_loop(0, groups, charge_group, 0)

    to_sib.wait_recv()
    for j in range(PIECES):

        @pl.when(has_prev)
        def _():
            prev_to_sib(j).wait_recv()
            prev_to_edge(j).wait_recv()

    first_local = (c - 1) * per_dev
    total = per_dev * n_clus

    def place_of(cluster, slot):
        at = neighbours[cluster, slot]
        if total & (total - 1) == 0:
            to = (at - first_local) & (total - 1)
        else:
            to = lax.rem(at - first_local + total, total)
        return jnp.where(at < 0, 3 * per_dev, jnp.minimum(to, 3 * per_dev))

    def stores(group):
        place = pl.ds(group * GROUP, GROUP)
        return (
            pltpu.make_async_copy(res.at[place], res_hbm.at[place], store_sem.at[0, group]),
            pltpu.make_async_copy(upd.at[place], upd_hbm.at[place], store_sem.at[1, group]),
        )

    def sweep_group(group, carry):
        first = group * GROUP
        for k in range(slots):
            for n in range(0, GROUP, 2):
                one = ext[place_of(first + n, k)]
                two = ext[place_of(first + n + 1, k)]
                both = jnp.concatenate([one, two], axis=1)
                out = jnp.dot(toep[k], both, preferred_element_type=jnp.float32)
                out = out.astype(jnp.bfloat16)
                lanes = pl.ds(k * unknowns, unknowns)
                filt[pl.ds(n * steps, steps), lanes] = out[:, :unknowns]
                filt[pl.ds((n + 1) * steps, steps), lanes] = out[:, unknowns:]
        near = jnp.dot(filt[...], coup[...], preferred_element_type=jnp.float32)
        place = pl.ds(first, GROUP)
        residual = base[place] - near.reshape(GROUP, steps, unknowns)
        res[place] = residual
        rounded = residual.astype(jnp.bfloat16)
        rows = ext[pl.ds(per_dev + first, GROUP), pl.ds(lags, steps)]
        for n in range(GROUP):
            step = jnp.dot(rounded[n], binv[first + n], preferred_element_type=jnp.float32)
            upd[first + n] = (rows[n].astype(jnp.float32) + step).astype(upd.dtype)
        for store in stores(group):
            store.start()
        return carry

    lax.fori_loop(0, groups, sweep_group, 0)

    to_sib.wait_send()
    for by in range(1, n_tm):

        @pl.when(i + by < n_tm)
        def _():
            total_to(by).wait_send()

    for j in range(PIECES):
        to_edge(j).wait_send()

        @pl.when(has_later)
        def _():
            to_later(j).wait_send()

        @pl.when(has_prev)
        def _():
            prev_to_sib(j).wait_send()

        @pl.when(has_prev & jnp.logical_not(wraps))
        def _():
            prev_to_edge(j).wait_send()

        @pl.when(wraps & has_later)
        def _():
            edge_to_later(j).wait_send()

    for group in range(groups):
        for store in stores(group):
            store.wait()


def on_device(
    currents, excitation, neighbours, lag_profile, couplings, block_inverses, charge_map, potential
):
    per_dev, steps, unknowns = currents.shape
    slots, lags = lag_profile.shape
    window = steps + lags
    patches = charge_map.shape[1]
    n_tm, n_clus = lax.axis_size("tm"), lax.axis_size("clus")
    vmem = pl.BlockSpec(memory_space=pltpu.VMEM)
    smem = pl.BlockSpec(memory_space=pltpu.SMEM)
    anywhere = pl.BlockSpec(memory_space=pl.ANY)
    size = GROUP * steps
    pairs = per_dev * slots * steps * unknowns
    bf16, f32 = jnp.bfloat16, jnp.float32
    return pl.pallas_call(
        functools.partial(sweep_kernel, n_tm, n_clus),
        in_specs=[anywhere] * 4 + [smem, vmem, vmem, vmem],
        out_specs=[anywhere, anywhere],
        out_shape=[
            jax.ShapeDtypeStruct(currents.shape, bf16),
            jax.ShapeDtypeStruct(currents.shape, f32),
        ],
        scratch_shapes=[
            pltpu.VMEM((3 * per_dev + 1, window, unknowns), bf16),
            pltpu.VMEM((size, slots * unknowns), bf16),
            pltpu.VMEM((slots, steps, window), bf16),
            pltpu.VMEM((size, size), bf16),
            pltpu.VMEM((slots * unknowns, unknowns), bf16),
            pltpu.VMEM(block_inverses.shape, bf16),
            pltpu.VMEM(excitation.shape, bf16),
            pltpu.VMEM(currents.shape, f32),
            pltpu.VMEM(currents.shape, bf16),
            pltpu.VMEM(currents.shape, f32),
            pltpu.VMEM((per_dev, patches), f32),
            pltpu.VMEM((n_tm + 1, per_dev, patches), f32),
            pltpu.SemaphoreType.DMA((6, PIECES)),
            pltpu.SemaphoreType.DMA((1,)),
            pltpu.SemaphoreType.DMA((PIECES,)),
            pltpu.SemaphoreType.DMA((PIECES,)),
            pltpu.SemaphoreType.DMA((PIECES,)),
            pltpu.SemaphoreType.DMA((PIECES,)),
            pltpu.SemaphoreType.DMA((n_tm,)),
            pltpu.SemaphoreType.DMA((n_tm,)),
            pltpu.SemaphoreType.DMA((4,)),
            pltpu.SemaphoreType.DMA((2, per_dev // GROUP)),
        ],
        compiler_params=pltpu.CompilerParams(
            collective_id=0, has_side_effects=True, vmem_limit_bytes=56 << 20
        ),
        cost_estimate=pl.CostEstimate(
            flops=2 * pairs * (window + unknowns), bytes_accessed=8 << 20, transcendentals=0
        ),
    )(
        currents, excitation, couplings.reshape(slots * unknowns, unknowns), block_inverses,
        neighbours, charge_map, potential, lag_profile,
    )


def solution(mesh):
    in_specs = (
        P("clus", "tm", None),
        P("clus", "tm", None),
        P("clus", None),
        P(),
        P(),
        P("clus", None, None),
        P(),
        P(),
    )
    out_specs = (P("clus", "tm", None), P("clus", "tm", None))
    return jax.shard_map(
        on_device, mesh=mesh, in_specs=in_specs, out_specs=out_specs, check_vma=False
    )
```

time: 45.2 us -> 43.1 us (0.954)
  Pallas kernels: 44.3 us -> 39.3 us
  local copies, waits for them, and re-layouts: 0 us -> 2.93 us
    pallas_call x2 -> x1, Pallas kernels: 44.3 us -> 39.3 us  [on_device(): pl.pallas_call(functools.partial(sweep_kernel, n_tm, n_clus), in_specs=[a...]
    unnamed x0 -> x4, local copies, waits for them, and re-layouts: none -> 2.93 us
where the time goes in v4:
time: 43.1 us; the launch traced here: 42.9 us
  Pallas kernels  39.3 us (91%)
  local copies, waits for them, and re-layouts  2.93 us (7%)
  between operations  0.65 us (2%)
    pallas_call x1, Pallas kernels, on_device(): pl.pallas_call(functools.partial(sweep_kernel, n_tm, n_clus), in_specs=[a...  39.3 us
    unnamed x4, local copies, waits for them, and re-layouts  2.93 us

profile of v4, /device:TPU:5, one launch (start us, length us, event | category | flops | bytes accessed | tf_op | source)
XLA Modules:
  0.0 42.9 jit_solution(1025859111434426078)
XLA Ops:
  0.6 39.3 %shard_map.95 = (bf16[32,64,128]{2,1,0:T(8,128)(2,1)}, f32[32,64,128]{2,1,0:T(8,128)}) custom-call(bf16[32,64,128]{2,1,0:T(8,128)(2,1)} %own_hbm.1, bf16[32,64,128]{2,1,0:T(8,128)(2,1)} %exc_hbm.1, bf16[3840,128]{1,0:T(8,128)(2,1)} %bitcast.1, bf16[32,128,128]{2,1,0:T(8,128)(2,1)} %binv_hbm.1, s32[32,30]{1,0:T(8,128)} %neighbours.1, bf16[128,128]{1,0:T(8,128)(2,1)} %cmap.1, ...), custom_call_target="tpu_custom_call" | custom-call | flops 4026531840 | bytes 8388608 | tf_op jit(solution)/shard_map/pallas_call | solution.py:297
  40.0 0.0 copy-start
  40.0 2.0 %copy.12 = bf16[32,64,128]{2,1,0:T(8,128)(2,1)} copy(bf16[32,64,128]{2,1,0:T(8,128)(2,1)} %get-tuple-element.4) | data formatting | bytes 1048576
  41.9 0.0 copy-done
  41.9 1.0 %copy.13 = f32[32,64,128]{2,1,0:T(8,128)} copy(f32[32,64,128]{2,1,0:T(8,128)S(1)} %copy-done) | data formatting | bytes 2097152
Async XLA Ops:
  40.0 2.0 %copy-start = (f32[32,64,128]{2,1,0:T(8,128)S(1)}, f32[32,64,128]{2,1,0:T(8,128)}, u32[]{:S(2)}) copy-start(f32[32,64,128]{2,1,0:T(8,128)} %get-tuple-element.5) | copy-start | bytes 3145732

commit v5 on v4

--- a/solution.py
+++ b/solution.py
@@ -7,15 +7,16 @@
 from jax.experimental.pallas import tpu as pltpu
 from jax.sharding import PartitionSpec as P
 
-GROUP = 4
+GROUP = 8
+CHARGE_GROUP = 4
 PIECES = 8
 MESH = pl.DeviceIdType.MESH
 
 
 def sweep_kernel(
     n_tm, n_clus, own_hbm, exc_hbm, coup_hbm, binv_hbm, neighbours, cmap, pot, profile,
-    upd_hbm, res_hbm,
-    ext, filt, toep, lower, coup, binv, exc, base, upd, res, before, totals,
+    corr_hbm, fields_hbm,
+    ext, filt, toep, lower, coup, binv, exc, base, corr, fields, before, totals,
     send, sib_sem, edge_sem, prev_sem, sib_prev_sem, edge_prev_sem, total_send, total_recv,
     load_sem, store_sem,
 ):
@@ -25,7 +26,7 @@
     lags = profile.shape[1]
     patches = cmap.shape[1]
     groups = per_dev // GROUP
-    size = GROUP * steps
+    size = CHARGE_GROUP * steps
     core = lax.rem(c, 2)
     sibling = c + 1 - 2 * core
     beyond = lax.rem(c + 2 * core - 1 + n_clus, n_clus)
@@ -33,6 +34,14 @@
     has_prev, has_later = i > 0, i < n_tm - 1
     later = lax.rem(i + 1, n_tm)
     piece = per_dev // PIECES
+    even = lax.rem(i, 2) == 0
+
+    def wrap_over_tm(j):
+        return wraps & has_later & (even | (j < PIECES // 2))
+
+    def prev_over_clus(j):
+        return has_prev & (jnp.logical_not(wraps) | (even & (j >= PIECES // 2)))
+
     from_beyond, from_sibling = 2 * core, 2 - 2 * core
 
     barrier = pltpu.get_barrier_semaphore()
@@ -156,11 +165,11 @@
 
         to_edge(j).wait_recv()
 
-        @pl.when(has_prev & jnp.logical_not(wraps))
+        @pl.when(prev_over_clus(j))
         def _():
             prev_to_edge(j).start()
 
-        @pl.when(wraps & has_later)
+        @pl.when(wrap_over_tm(j))
         def _():
             edge_to_later(j).start()
 
@@ -176,25 +185,23 @@
         load.wait()
 
     def charge_group(group, carry):
-        first = group * GROUP
-        rows = ext[pl.ds(per_dev + first, GROUP), pl.ds(lags, steps)].reshape(size, unknowns)
+        first = group * CHARGE_GROUP
+        rows = ext[pl.ds(per_dev + first, CHARGE_GROUP), pl.ds(lags, steps)].reshape(size, unknowns)
         incr = jnp.dot(rows, cmap[...], preferred_element_type=jnp.float32)
         high = incr.astype(jnp.bfloat16)
         rest = (incr - high.astype(jnp.float32)).astype(jnp.bfloat16)
         sums = jnp.dot(
             lower[...], jnp.concatenate([high, rest], axis=1), preferred_element_type=jnp.float32
         )
-        running = (sums[:, :patches] + sums[:, patches:]).reshape(GROUP, steps, patches)
-        charge = (running + before[pl.ds(first, GROUP)][:, None, :]).astype(jnp.bfloat16)
+        running = (sums[:, :patches] + sums[:, patches:]).reshape(CHARGE_GROUP, steps, patches)
+        charge = (running + before[pl.ds(first, CHARGE_GROUP)][:, None, :]).astype(jnp.bfloat16)
         field = jnp.dot(
             charge.reshape(size, patches), pot[...], preferred_element_type=jnp.float32
         )
-        field = field.reshape(GROUP, steps, unknowns)
-        place = pl.ds(first, GROUP)
-        base[place] = exc[place].astype(jnp.float32) - field
+        base[pl.ds(first, CHARGE_GROUP)] = field.reshape(CHARGE_GROUP, steps, unknowns)
         return carry
 
-    lax.fori_loop(0, groups, charge_group, 0)
+    lax.fori_loop(0, per_dev // CHARGE_GROUP, charge_group, 0)
 
     to_sib.wait_recv()
     for j in range(PIECES):
@@ -218,8 +225,8 @@
     def stores(group):
         place = pl.ds(group * GROUP, GROUP)
         return (
-            pltpu.make_async_copy(res.at[place], res_hbm.at[place], store_sem.at[0, group]),
-            pltpu.make_async_copy(upd.at[place], upd_hbm.at[place], store_sem.at[1, group]),
+            pltpu.make_async_copy(fields.at[place], fields_hbm.at[place], store_sem.at[0, group]),
+            pltpu.make_async_copy(corr.at[place], corr_hbm.at[place], store_sem.at[1, group]),
         )
 
     def sweep_group(group, carry):
@@ -236,13 +243,13 @@
                 filt[pl.ds((n + 1) * steps, steps), lanes] = out[:, unknowns:]
         near = jnp.dot(filt[...], coup[...], preferred_element_type=jnp.float32)
         place = pl.ds(first, GROUP)
-        residual = base[place] - near.reshape(GROUP, steps, unknowns)
-        res[place] = residual
-        rounded = residual.astype(jnp.bfloat16)
-        rows = ext[pl.ds(per_dev + first, GROUP), pl.ds(lags, steps)]
+        both_fields = base[place] + near.reshape(GROUP, steps, unknowns)
+        fields[place] = both_fields
+        rounded = (exc[place].astype(jnp.float32) - both_fields).astype(jnp.bfloat16)
         for n in range(GROUP):
-            step = jnp.dot(rounded[n], binv[first + n], preferred_element_type=jnp.float32)
-            upd[first + n] = (rows[n].astype(jnp.float32) + step).astype(upd.dtype)
+            corr[first + n] = jnp.dot(
+                rounded[n], binv[first + n], preferred_element_type=jnp.float32
+            )
         for store in stores(group):
             store.start()
         return carry
@@ -267,11 +274,11 @@
         def _():
             prev_to_sib(j).wait_send()
 
-        @pl.when(has_prev & jnp.logical_not(wraps))
+        @pl.when(prev_over_clus(j))
         def _():
             prev_to_edge(j).wait_send()
 
-        @pl.when(wraps & has_later)
+        @pl.when(wrap_over_tm(j))
         def _():
             edge_to_later(j).wait_send()
 
@@ -291,27 +298,27 @@
     vmem = pl.BlockSpec(memory_space=pltpu.VMEM)
     smem = pl.BlockSpec(memory_space=pltpu.SMEM)
     anywhere = pl.BlockSpec(memory_space=pl.ANY)
-    size = GROUP * steps
+    size = CHARGE_GROUP * steps
     pairs = per_dev * slots * steps * unknowns
     bf16, f32 = jnp.bfloat16, jnp.float32
-    return pl.pallas_call(
+    correction, fields = pl.pallas_call(
         functools.partial(sweep_kernel, n_tm, n_clus),
         in_specs=[anywhere] * 4 + [smem, vmem, vmem, vmem],
         out_specs=[anywhere, anywhere],
         out_shape=[
-            jax.ShapeDtypeStruct(currents.shape, bf16),
+            jax.ShapeDtypeStruct(currents.shape, f32),
             jax.ShapeDtypeStruct(currents.shape, f32),
         ],
         scratch_shapes=[
             pltpu.VMEM((3 * per_dev + 1, window, unknowns), bf16),
-            pltpu.VMEM((size, slots * unknowns), bf16),
+            pltpu.VMEM((GROUP * steps, slots * unknowns), bf16),
             pltpu.VMEM((slots, steps, window), bf16),
             pltpu.VMEM((size, size), bf16),
             pltpu.VMEM((slots * unknowns, unknowns), bf16),
             pltpu.VMEM(block_inverses.shape, bf16),
             pltpu.VMEM(excitation.shape, bf16),
             pltpu.VMEM(currents.shape, f32),
-            pltpu.VMEM(currents.shape, bf16),
+            pltpu.VMEM(currents.shape, f32),
             pltpu.VMEM(currents.shape, f32),
             pltpu.VMEM((per_dev, patches), f32),
             pltpu.VMEM((n_tm + 1, per_dev, patches), f32),
@@ -336,6 +343,9 @@
         currents, excitation, couplings.reshape(slots * unknowns, unknowns), block_inverses,
         neighbours, charge_map, potential, lag_profile,
     )
+    residual = excitation.astype(f32) - fields
+    updated = (currents.astype(f32) + correction).astype(bf16)
+    return (updated, residual)
 
 
 def solution(mesh):

time: 43.1 us -> 40.9 us (0.949)
  other arithmetic: 0 us -> 3.05 us
  local copies, waits for them, and re-layouts: 2.93 us -> 0.01 us
  Pallas kernels: 39.3 us -> 37 us
    sub x0 -> x1, other arithmetic: none -> 3.05 us  [on_device(): residual = excitation.astype(f32) - fields]
    unnamed x4, local copies, waits for them, and re-layouts: 2.93 us -> 0.01 us
    pallas_call x1, Pallas kernels: 39.3 us -> 37 us  [on_device(): pl.pallas_call(functools.partial(sweep_kernel, n_tm, n_clus), in_specs=[a...]
where the time goes in v5:
time: 40.9 us; the launch traced here: 40.8 us
  Pallas kernels  37 us (90%)
  other arithmetic  3.05 us (7%)
  between operations  0.67 us (2%)
    pallas_call x1, Pallas kernels, on_device(): pl.pallas_call(functools.partial(sweep_kernel, n_tm, n_clus), in_specs=[a...  37 us
    sub x1, other arithmetic, on_device(): residual = excitation.astype(f32) - fields  3.05 us

profile of v5, /device:TPU:5, one launch (start us, length us, event | category | flops | bytes accessed | tf_op | source)
XLA Modules:
  0.0 40.8 jit_solution(13278627346094555419)
XLA Ops:
  0.6 0.0 copy-start
  0.6 0.0 copy-start.1
  0.7 37.0 %shard_map.95 = (f32[32,64,128]{2,1,0:T(8,128)}, f32[32,64,128]{2,1,0:T(8,128)}) custom-call(bf16[32,64,128]{2,1,0:T(8,128)(2,1)} %own_hbm.1, bf16[32,64,128]{2,1,0:T(8,128)(2,1)} %exc_hbm.1, bf16[3840,128]{1,0:T(8,128)(2,1)} %bitcast.1, bf16[32,128,128]{2,1,0:T(8,128)(2,1)} %binv_hbm.1, s32[32,30]{1,0:T(8,128)} %neighbours.1, bf16[128,128]{1,0:T(8,128)(2,1)} %cmap.1, ...), custom_call_target="tpu_custom_call" | custom-call | flops 4026531840 | bytes 8388608 | tf_op jit(solution)/shard_map/pallas_call | solution.py:304
  37.7 0.0 copy-done
  37.7 0.0 copy-done.1
  37.7 3.1 %convert_subtract_fusion = (f32[32,64,128]{2,1,0:T(8,128)}, bf16[32,64,128]{2,1,0:T(8,128)(2,1)}) fusion(f32[32,64,128]{2,1,0:T(8,128)} %get-tuple-element.5, bf16[32,64,128]{2,1,0:T(8,128)(2,1)S(1)} %copy-done.1, f32[32,64,128]{2,1,0:T(8,128)} %get-tuple-element.4, bf16[32,64,128]{2,1,0:T(8,128)(2,1)S(1)} %copy-done), kind=kLoop, calls=%fused_computation | loop fusion | flops 1310720 | bytes 4718592 | tf_op jit(solution)/shard_map/sub | solution.py:346
Async XLA Ops:
  0.6 37.0 %copy-start = (bf16[32,64,128]{2,1,0:T(8,128)(2,1)S(1)}, bf16[32,64,128]{2,1,0:T(8,128)(2,1)}, u32[]{:S(2)}) copy-start(bf16[32,64,128]{2,1,0:T(8,128)(2,1)} %own_hbm.1) | copy-start | bytes 1572868
  0.6 37.0 %copy-start.1 = (bf16[32,64,128]{2,1,0:T(8,128)(2,1)S(1)}, bf16[32,64,128]{2,1,0:T(8,128)(2,1)}, u32[]{:S(2)}) copy-start(bf16[32,64,128]{2,1,0:T(8,128)(2,1)} %exc_hbm.1) | copy-start | bytes 1572868

commit v6 on v5

--- a/solution.py
+++ b/solution.py
@@ -15,10 +15,10 @@
 
 def sweep_kernel(
     n_tm, n_clus, own_hbm, exc_hbm, coup_hbm, binv_hbm, neighbours, cmap, pot, profile,
-    corr_hbm, fields_hbm,
-    ext, filt, toep, lower, coup, binv, exc, base, corr, fields, before, totals,
+    corr, fields,
+    ext, filt, toep, lower, coup, binv, exc, base, before, totals,
     send, sib_sem, edge_sem, prev_sem, sib_prev_sem, edge_prev_sem, total_send, total_recv,
-    load_sem, store_sem,
+    load_sem,
 ):
     i, c = lax.axis_index("tm"), lax.axis_index("clus")
     per_dev, steps, unknowns = own_hbm.shape
@@ -37,10 +37,10 @@
     even = lax.rem(i, 2) == 0
 
     def wrap_over_tm(j):
-        return wraps & has_later & (even | (j < PIECES // 2))
+        return wraps & has_later & (even | (j < 5 * PIECES // 8))
 
     def prev_over_clus(j):
-        return has_prev & (jnp.logical_not(wraps) | (even & (j >= PIECES // 2)))
+        return has_prev & (jnp.logical_not(wraps) | (even & (j >= 5 * PIECES // 8)))
 
     from_beyond, from_sibling = 2 * core, 2 - 2 * core
 
@@ -221,13 +221,6 @@
         else:
             to = lax.rem(at - first_local + total, total)
         return jnp.where(at < 0, 3 * per_dev, jnp.minimum(to, 3 * per_dev))
-
-    def stores(group):
-        place = pl.ds(group * GROUP, GROUP)
-        return (
-            pltpu.make_async_copy(fields.at[place], fields_hbm.at[place], store_sem.at[0, group]),
-            pltpu.make_async_copy(corr.at[place], corr_hbm.at[place], store_sem.at[1, group]),
-        )
 
     def sweep_group(group, carry):
         first = group * GROUP
@@ -250,8 +243,6 @@
             corr[first + n] = jnp.dot(
                 rounded[n], binv[first + n], preferred_element_type=jnp.float32
             )
-        for store in stores(group):
-            store.start()
         return carry
 
     lax.fori_loop(0, groups, sweep_group, 0)
@@ -281,10 +272,6 @@
         @pl.when(wrap_over_tm(j))
         def _():
             edge_to_later(j).wait_send()
-
-    for group in range(groups):
-        for store in stores(group):
-            store.wait()
 
 
 def on_device(
@@ -297,17 +284,17 @@
     n_tm, n_clus = lax.axis_size("tm"), lax.axis_size("clus")
     vmem = pl.BlockSpec(memory_space=pltpu.VMEM)
     smem = pl.BlockSpec(memory_space=pltpu.SMEM)
-    anywhere = pl.BlockSpec(memory_space=pl.ANY)
+    hbm = pl.BlockSpec(memory_space=pltpu.HBM)
     size = CHARGE_GROUP * steps
     pairs = per_dev * slots * steps * unknowns
     bf16, f32 = jnp.bfloat16, jnp.float32
     correction, fields = pl.pallas_call(
         functools.partial(sweep_kernel, n_tm, n_clus),
-        in_specs=[anywhere] * 4 + [smem, vmem, vmem, vmem],
-        out_specs=[anywhere, anywhere],
+        in_specs=[hbm] * 4 + [smem, vmem, vmem, vmem],
+        out_specs=[vmem, vmem],
         out_shape=[
-            jax.ShapeDtypeStruct(currents.shape, f32),
-            jax.ShapeDtypeStruct(currents.shape, f32),
+            pltpu.VMEM(currents.shape, f32),
+            pltpu.VMEM(currents.shape, f32),
         ],
         scratch_shapes=[
             pltpu.VMEM((3 * per_dev + 1, window, unknowns), bf16),
@@ -317,8 +304,6 @@
             pltpu.VMEM((slots * unknowns, unknowns), bf16),
             pltpu.VMEM(block_inverses.shape, bf16),
             pltpu.VMEM(excitation.shape, bf16),
-            pltpu.VMEM(currents.shape, f32),
-            pltpu.VMEM(currents.shape, f32),
             pltpu.VMEM(currents.shape, f32),
             pltpu.VMEM((per_dev, patches), f32),
             pltpu.VMEM((n_tm + 1, per_dev, patches), f32),
@@ -331,10 +316,9 @@
             pltpu.SemaphoreType.DMA((n_tm,)),
             pltpu.SemaphoreType.DMA((n_tm,)),
             pltpu.SemaphoreType.DMA((4,)),
-            pltpu.SemaphoreType.DMA((2, per_dev // GROUP)),
         ],
         compiler_params=pltpu.CompilerParams(
-            collective_id=0, has_side_effects=True, vmem_limit_bytes=56 << 20
+            collective_id=0, has_side_effects=True, vmem_limit_bytes=61 << 20
         ),
         cost_estimate=pl.CostEstimate(
             flops=2 * pairs * (window + unknowns), bytes_accessed=8 << 20, transcendentals=0

time: 40.9 us -> 39 us (0.954)
  Pallas kernels: 37 us -> 35.6 us
  other arithmetic: 3.05 us -> 2.56 us
    pallas_call x1, Pallas kernels: 37 us -> 35.6 us  [on_device(): pl.pallas_call(functools.partial(sweep_kernel, n_tm, n_clus), in_specs=[h...]
    sub x1, other arithmetic: 3.05 us -> 2.56 us  [on_device(): residual = excitation.astype(f32) - fields]
where the time goes in v6:
time: 39 us; the launch traced here: 38.8 us
  Pallas kernels  35.6 us (91%)
  other arithmetic  2.56 us (7%)
  between operations  0.66 us (2%)
    pallas_call x1, Pallas kernels, on_device(): pl.pallas_call(functools.partial(sweep_kernel, n_tm, n_clus), in_specs=[h...  35.6 us
    sub x1, other arithmetic, on_device(): residual = excitation.astype(f32) - fields  2.56 us

profile of v6, /device:TPU:5, one launch (start us, length us, event | category | flops | bytes accessed | tf_op | source)
XLA Modules:
  0.0 38.8 jit_solution(1739154968473214517)
XLA Ops:
  0.6 0.0 copy-start
  0.6 35.6 %shard_map.95 = (f32[32,64,128]{2,1,0:T(8,128)S(1)}, f32[32,64,128]{2,1,0:T(8,128)S(1)}) custom-call(bf16[32,64,128]{2,1,0:T(8,128)(2,1)} %own_hbm.1, bf16[32,64,128]{2,1,0:T(8,128)(2,1)} %exc_hbm.1, bf16[3840,128]{1,0:T(8,128)(2,1)} %bitcast.1, bf16[32,128,128]{2,1,0:T(8,128)(2,1)} %binv_hbm.1, s32[32,30]{1,0:T(8,128)} %neighbours.1, ...), custom_call_target="tpu_custom_call" | custom-call | flops 4026531840 | bytes 8388608 | tf_op jit(solution)/shard_map/pallas_call | solution.py:291
  36.3 0.0 copy-done
  36.3 2.6 %convert_subtract_fusion = (f32[32,64,128]{2,1,0:T(8,128)}, bf16[32,64,128]{2,1,0:T(8,128)(2,1)}) fusion(f32[32,64,128]{2,1,0:T(8,128)S(1)} %get-tuple-element.5, bf16[32,64,128]{2,1,0:T(8,128)(2,1)} %exc_hbm.1, f32[32,64,128]{2,1,0:T(8,128)S(1)} %get-tuple-element.4, bf16[32,64,128]{2,1,0:T(8,128)(2,1)S(1)} %copy-done), kind=kLoop, calls=%fused_computation | loop fusion | flops 1310720 | bytes 4718592 | tf_op jit(solution)/shard_map/sub | solution.py:330
Async XLA Ops:
  0.6 35.6 %copy-start = (bf16[32,64,128]{2,1,0:T(8,128)(2,1)S(1)}, bf16[32,64,128]{2,1,0:T(8,128)(2,1)}, u32[]{:S(2)}) copy-start(bf16[32,64,128]{2,1,0:T(8,128)(2,1)} %own_hbm.1) | copy-start | bytes 1572868

commit v7 on v6

--- a/solution.py
+++ b/solution.py
@@ -7,7 +7,7 @@
 from jax.experimental.pallas import tpu as pltpu
 from jax.sharding import PartitionSpec as P
 
-GROUP = 8
+GROUP = 16
 CHARGE_GROUP = 4
 PIECES = 8
 MESH = pl.DeviceIdType.MESH
@@ -15,7 +15,7 @@
 
 def sweep_kernel(
     n_tm, n_clus, own_hbm, exc_hbm, coup_hbm, binv_hbm, neighbours, cmap, pot, profile,
-    corr, fields,
+    upd, res,
     ext, filt, toep, lower, coup, binv, exc, base, before, totals,
     send, sib_sem, edge_sem, prev_sem, sib_prev_sem, edge_prev_sem, total_send, total_recv,
     load_sem,
@@ -198,7 +198,9 @@
         field = jnp.dot(
             charge.reshape(size, patches), pot[...], preferred_element_type=jnp.float32
         )
-        base[pl.ds(first, CHARGE_GROUP)] = field.reshape(CHARGE_GROUP, steps, unknowns)
+        place = pl.ds(first, CHARGE_GROUP)
+        field = field.reshape(CHARGE_GROUP, steps, unknowns)
+        base[place] = exc[place].astype(jnp.float32) - field
         return carry
 
     lax.fori_loop(0, per_dev // CHARGE_GROUP, charge_group, 0)
@@ -236,13 +238,13 @@
                 filt[pl.ds((n + 1) * steps, steps), lanes] = out[:, unknowns:]
         near = jnp.dot(filt[...], coup[...], preferred_element_type=jnp.float32)
         place = pl.ds(first, GROUP)
-        both_fields = base[place] + near.reshape(GROUP, steps, unknowns)
-        fields[place] = both_fields
-        rounded = (exc[place].astype(jnp.float32) - both_fields).astype(jnp.bfloat16)
+        residual = base[place] - near.reshape(GROUP, steps, unknowns)
+        res[place] = residual
+        rounded = residual.astype(jnp.bfloat16)
+        rows = ext[pl.ds(per_dev + first, GROUP), pl.ds(lags, steps)]
         for n in range(GROUP):
-            corr[first + n] = jnp.dot(
-                rounded[n], binv[first + n], preferred_element_type=jnp.float32
-            )
+            step = jnp.dot(rounded[n], binv[first + n], preferred_element_type=jnp.float32)
+            upd[first + n] = (rows[n].astype(jnp.float32) + step).astype(upd.dtype)
         return carry
 
     lax.fori_loop(0, groups, sweep_group, 0)
@@ -288,12 +290,12 @@
     size = CHARGE_GROUP * steps
     pairs = per_dev * slots * steps * unknowns
     bf16, f32 = jnp.bfloat16, jnp.float32
-    correction, fields = pl.pallas_call(
+    return pl.pallas_call(
         functools.partial(sweep_kernel, n_tm, n_clus),
         in_specs=[hbm] * 4 + [smem, vmem, vmem, vmem],
         out_specs=[vmem, vmem],
         out_shape=[
-            pltpu.VMEM(currents.shape, f32),
+            pltpu.VMEM(currents.shape, bf16),
             pltpu.VMEM(currents.shape, f32),
         ],
         scratch_shapes=[
@@ -327,9 +329,6 @@
         currents, excitation, couplings.reshape(slots * unknowns, unknowns), block_inverses,
         neighbours, charge_map, potential, lag_profile,
     )
-    residual = excitation.astype(f32) - fields
-    updated = (currents.astype(f32) + correction).astype(bf16)
-    return (updated, residual)
 
 
 def solution(mesh):

time: 39 us -> 37.5 us (0.962)
  other arithmetic: 2.56 us -> 0 us
  local copies, waits for them, and re-layouts: 0.01 us -> 1.77 us
  Pallas kernels: 35.6 us -> 34.9 us
    sub x1 -> x0, other arithmetic: 2.56 us -> none  [on_device(): residual = excitation.astype(f32) - fields]
    unnamed x2, local copies, waits for them, and re-layouts: 0.01 us -> 1.77 us
    pallas_call x1, Pallas kernels: 35.6 us -> 34.9 us  [on_device(): pl.pallas_call(functools.partial(sweep_kernel, n_tm, n_clus), in_specs=[h...]
where the time goes in v7:
time: 37.5 us; the launch traced here: 37.3 us
  Pallas kernels  34.9 us (93%)
  local copies, waits for them, and re-layouts  1.77 us (5%)
  between operations  0.64 us (2%)
    pallas_call x1, Pallas kernels, on_device(): pl.pallas_call(functools.partial(sweep_kernel, n_tm, n_clus), in_specs=[h...  34.9 us
    unnamed x2, local copies, waits for them, and re-layouts  1.77 us

profile of v7, /device:TPU:5, one launch (start us, length us, event | category | flops | bytes accessed | tf_op | source)
XLA Modules:
  0.0 37.3 jit_solution(6857687396558737850)
XLA Ops:
  0.6 34.9 %shard_map.95 = (bf16[32,64,128]{2,1,0:T(8,128)(2,1)S(1)}, f32[32,64,128]{2,1,0:T(8,128)S(1)}) custom-call(bf16[32,64,128]{2,1,0:T(8,128)(2,1)} %own_hbm.1, bf16[32,64,128]{2,1,0:T(8,128)(2,1)} %exc_hbm.1, bf16[3840,128]{1,0:T(8,128)(2,1)} %bitcast.1, bf16[32,128,128]{2,1,0:T(8,128)(2,1)} %binv_hbm.1, s32[32,30]{1,0:T(8,128)} %neighbours.1, ...), custom_call_target="tpu_custom_call" | custom-call | flops 4026531840 | bytes 8388608 | tf_op jit(solution)/shard_map/pallas_call | solution.py:293
  35.5 0.8 %copy.12 = bf16[32,64,128]{2,1,0:T(8,128)(2,1)} copy(bf16[32,64,128]{2,1,0:T(8,128)(2,1)S(1)} %get-tuple-element.2) | data formatting | bytes 1048576
  36.3 1.0 %copy.13 = f32[32,64,128]{2,1,0:T(8,128)} copy(f32[32,64,128]{2,1,0:T(8,128)S(1)} %get-tuple-element.3) | data formatting | bytes 2097152

commit v8 on v7

--- a/solution.py
+++ b/solution.py
@@ -37,10 +37,10 @@
     even = lax.rem(i, 2) == 0
 
     def wrap_over_tm(j):
-        return wraps & has_later & (even | (j < 5 * PIECES // 8))
+        return wraps & has_later & (even | (j < 3 * PIECES // 4))
 
     def prev_over_clus(j):
-        return has_prev & (jnp.logical_not(wraps) | (even & (j >= 5 * PIECES // 8)))
+        return has_prev & (jnp.logical_not(wraps) | (even & (j >= 3 * PIECES // 4)))
 
     from_beyond, from_sibling = 2 * core, 2 - 2 * core
 
@@ -156,23 +156,6 @@
     keep = (row >= col) & (row // steps == col // steps)
     lower[...] = jnp.where(keep, 1.0, 0.0).astype(lower.dtype)
 
-    for j in range(PIECES):
-
-        @pl.when(has_prev)
-        def _():
-            to_later(j).wait_recv()
-            prev_to_sib(j).start()
-
-        to_edge(j).wait_recv()
-
-        @pl.when(prev_over_clus(j))
-        def _():
-            prev_to_edge(j).start()
-
-        @pl.when(wrap_over_tm(j))
-        def _():
-            edge_to_later(j).start()
-
     before[...] = jnp.zeros(before.shape, before.dtype)
     for by in range(1, n_tm):
 
@@ -184,7 +167,7 @@
     for load in loads:
         load.wait()
 
-    def charge_group(group, carry):
+    def charge_group(group):
         first = group * CHARGE_GROUP
         rows = ext[pl.ds(per_dev + first, CHARGE_GROUP), pl.ds(lags, steps)].reshape(size, unknowns)
         incr = jnp.dot(rows, cmap[...], preferred_element_type=jnp.float32)
@@ -201,9 +184,26 @@
         place = pl.ds(first, CHARGE_GROUP)
         field = field.reshape(CHARGE_GROUP, steps, unknowns)
         base[place] = exc[place].astype(jnp.float32) - field
-        return carry
-
-    lax.fori_loop(0, per_dev // CHARGE_GROUP, charge_group, 0)
+
+    for j in range(PIECES):
+
+        @pl.when(has_prev)
+        def _():
+            to_later(j).wait_recv()
+            prev_to_sib(j).start()
+
+        to_edge(j).wait_recv()
+
+        @pl.when(prev_over_clus(j))
+        def _():
+            prev_to_edge(j).start()
+
+        @pl.when(wrap_over_tm(j))
+        def _():
+            edge_to_later(j).start()
+
+        for group in range(j, per_dev // CHARGE_GROUP, PIECES):
+            charge_group(group)
 
     to_sib.wait_recv()
     for j in range(PIECES):

time: 37.5 us -> 40 us (1.067)
  Pallas kernels: 34.9 us -> 37.4 us
    pallas_call x1, Pallas kernels: 34.9 us -> 37.4 us  [on_device(): pl.pallas_call(functools.partial(sweep_kernel, n_tm, n_clus), in_specs=[h...]
where the time goes in v8:
time: 40 us; the launch traced here: 39.8 us
  Pallas kernels  37.4 us (94%)
  local copies, waits for them, and re-layouts  1.77 us (4%)
  between operations  0.64 us (2%)
    pallas_call x1, Pallas kernels, on_device(): pl.pallas_call(functools.partial(sweep_kernel, n_tm, n_clus), in_specs=[h...  37.4 us
    unnamed x2, local copies, waits for them, and re-layouts  1.77 us

profile of v8, /device:TPU:5, one launch (start us, length us, event | category | flops | bytes accessed | tf_op | source)
XLA Modules:
  0.0 39.8 jit_solution(14426757706349536577)
XLA Ops:
  0.6 37.4 %shard_map.95 = (bf16[32,64,128]{2,1,0:T(8,128)(2,1)S(1)}, f32[32,64,128]{2,1,0:T(8,128)S(1)}) custom-call(bf16[32,64,128]{2,1,0:T(8,128)(2,1)} %own_hbm.1, bf16[32,64,128]{2,1,0:T(8,128)(2,1)} %exc_hbm.1, bf16[3840,128]{1,0:T(8,128)(2,1)} %bitcast.1, bf16[32,128,128]{2,1,0:T(8,128)(2,1)} %binv_hbm.1, s32[32,30]{1,0:T(8,128)} %neighbours.1, ...), custom_call_target="tpu_custom_call" | custom-call | flops 4026531840 | bytes 8388608 | tf_op jit(solution)/shard_map/pallas_call | solution.py:293
  38.0 0.8 %copy.12 = bf16[32,64,128]{2,1,0:T(8,128)(2,1)} copy(bf16[32,64,128]{2,1,0:T(8,128)(2,1)S(1)} %get-tuple-element.2) | data formatting | bytes 1048576
  38.8 1.0 %copy.13 = f32[32,64,128]{2,1,0:T(8,128)} copy(f32[32,64,128]{2,1,0:T(8,128)S(1)} %get-tuple-element.3) | data formatting | bytes 2097152
